TPU v7x, 128 devices: a whole 4x4x4 slice. The times are simulated.
128 devices in a mesh: seq: 8 (over z_hi, x), tp: 16 (over y, z_lo, core).
Axes of the slice: x: 4, y: 4, z: 4 (z_hi: 2, z_lo: 2; z = z_hi * 2 + z_lo), core: 2. Of those that a mesh axis runs over, the one named last changes fastest.
Arguments:
- activations: bfloat16 [2048, 8192], P('seq', 'tp'), may hold values from -36 to 36
- norm_gain: bfloat16 [8192], P('tp'), may hold values from 0.099609375 to 1.8984375
- in_proj: bfloat16 [8192, 3, 4096], P(None, None, 'tp'), may hold values from -0.0625 to 0.0625
- short_taps: float32 [3, 3, 4096], P(None, None, 'tp'), may hold values from -3.5 to 3.5
- medium_taps: float32 [256, 128], P('tp'), may hold values from -0.5 to 0.5
- cotangent: bfloat16 [2048, 4096], P('seq', 'tp'), may hold values from -1.1953125 to 1.1953125
Outputs:
- mixer_out: bfloat16 [2048, 4096], P('seq', 'tp')
- grad_input: bfloat16 [2048, 8192], P('seq', 'tp')
- grad_proj: bfloat16 [8192, 3, 4096], P('seq', None, 'tp')
All inputs are finite; a program needn't handle non-finite values.
Results may differ from a plain program's by a relative error of at most 0.02.
Values may be sent and summed in bfloat16 or wider, within the bound.
A program may use at most 192 MiB of HBM per device.

v0:
```python
import jax
import jax.numpy as jnp
from jax import lax
from jax.sharding import PartitionSpec as P

GROUP = 16
LS = 3
LM = 128


norm_eps = 1e-06


def shifted(block, axis, distance):
    devices = range(lax.axis_size(axis))
    route = [(i - distance, i) for i in devices if i - distance in devices]
    return lax.ppermute(block, axis, route)


def forward_short(source, taps, offset, length):
    total = jnp.zeros((length,) + source.shape[1:], jnp.float32)
    for index in range(LS):
        total = total + taps[index] * source[offset - index : offset - index + length].astype(
            jnp.float32
        )
    return total


def backward_short(source, taps, length):
    total = jnp.zeros((length,) + source.shape[1:], jnp.float32)
    for index in range(LS):
        total = total + taps[index] * source[index : index + length].astype(jnp.float32)
    return total


def band_matrix(tap_rows, out_len, in_len, lead, sign):
    offsets = lead + sign * (
        lax.broadcasted_iota(jnp.int32, (out_len, in_len), 0)
        - lax.broadcasted_iota(jnp.int32, (out_len, in_len), 1)
    )
    inside = (offsets >= 0) & (offsets < LM)
    picked = jnp.take(tap_rows, jnp.clip(offsets, 0, LM - 1), axis=1)
    return jnp.where(inside[None], picked, 0.0)


def grouped_apply(band, source):
    groups_here = band.shape[0]
    shaped = source.astype(jnp.float32).reshape(source.shape[0], groups_here, GROUP)
    result = jnp.einsum("gts,sgc->tgc", band, shaped, precision=lax.Precision.HIGHEST)
    return result.reshape(band.shape[1], groups_here * GROUP)


def per_device(activations, norm_gain, in_proj, short_taps, medium_taps, cotangent):
    act_full, gain_full = (
        lax.all_gather(activations, "tp", axis=1, tiled=True),
        lax.all_gather(norm_gain, "tp", axis=0, tiled=True),
    )
    tok_rows = act_full.shape[0]
    width = act_full.shape[1]
    local_ch = in_proj.shape[2]
    edge_rows = LM + LS - 2
    head_rows = LS - 1
    act_float = act_full.astype(jnp.float32)
    inv_rms = lax.rsqrt(jnp.mean(act_float * act_float, axis=1, keepdims=True) + norm_eps)
    gain_float = gain_full.astype(jnp.float32)
    normed = (act_float * inv_rms * gain_float).astype(jnp.bfloat16)
    weight = in_proj.reshape(width, 3 * local_ch)
    projected = (
        jnp.dot(normed, weight, preferred_element_type=jnp.float32)
        .astype(jnp.bfloat16)
        .reshape(tok_rows, 3, local_ch)
    )
    kv_tail = projected[tok_rows - edge_rows :, 1:, :].reshape(edge_rows, 2 * local_ch)
    q_tail = projected[tok_rows - head_rows :, 0, :].reshape(head_rows // 2, 2 * local_ch)
    received = shifted(jnp.concatenate([kv_tail, q_tail], 0), "seq", 1)
    kv_ext = jnp.concatenate(
        [received[:edge_rows].reshape(edge_rows, 2, local_ch), projected[:, 1:, :]], 0
    )
    q_ext = jnp.concatenate(
        [received[edge_rows:].reshape(head_rows, local_ch), projected[:, 0, :]], 0
    )
    span = tok_rows + LM - 1
    kv_feat = forward_short(kv_ext, short_taps[:, 1:, :], head_rows, span).astype(jnp.bfloat16)
    q_feat = forward_short(q_ext, short_taps[:, 0, :], head_rows, tok_rows).astype(jnp.bfloat16)
    gated = (kv_feat[:, 0].astype(jnp.float32) * kv_feat[:, 1].astype(jnp.float32)).astype(
        jnp.bfloat16
    )
    band_forward = band_matrix(medium_taps, tok_rows, span, LM - 1, 1)
    filtered = grouped_apply(band_forward, gated)
    mixer_out = (q_feat.astype(jnp.float32) * filtered).astype(jnp.bfloat16)
    grad_out = cotangent.astype(jnp.float32)
    grad_filtered = (grad_out * q_feat.astype(jnp.float32)).astype(jnp.bfloat16)
    grad_q = (grad_out * filtered).astype(jnp.bfloat16)
    kv_own = kv_feat[LM - 1 :]
    front = jnp.concatenate([grad_q[:head_rows, None, :], kv_own[:head_rows]], 1)
    outgoing = jnp.concatenate(
        [grad_filtered[:edge_rows], front.reshape(3 * head_rows, local_ch)], 0
    )
    returned = shifted(outgoing, "seq", -1)
    filt_ext = jnp.concatenate([grad_filtered, returned[:edge_rows]], 0)
    front_next = returned[edge_rows:].reshape(head_rows, 3, local_ch)
    reach = tok_rows + head_rows
    band_backward = band_matrix(medium_taps, reach, tok_rows + edge_rows, 0, -1)
    grad_gated = grouped_apply(band_backward, filt_ext)
    kv_reach = jnp.concatenate([kv_own, front_next[:, 1:, :]], 0)
    q_reach = jnp.concatenate([grad_q, front_next[:, 0, :]], 0)
    grad_k = (grad_gated * kv_reach[:, 1].astype(jnp.float32)).astype(jnp.bfloat16)
    grad_v = (grad_gated * kv_reach[:, 0].astype(jnp.float32)).astype(jnp.bfloat16)
    grad_feat = jnp.stack([q_reach, grad_k, grad_v], 1)
    grad_pre = (
        backward_short(grad_feat, short_taps, tok_rows)
        .astype(jnp.bfloat16)
        .reshape(tok_rows, 3 * local_ch)
    )
    partial_grad = lax.dot_general(
        grad_pre, weight, (((1,), (1,)), ((), ())), preferred_element_type=jnp.float32
    )
    tp_count = lax.axis_size("tp")
    own_width = width // tp_count
    own_scaled = activations.astype(jnp.float32) * inv_rms
    own_gain = norm_gain.astype(jnp.float32)
    whole_grad = lax.psum(partial_grad.astype(jnp.bfloat16), "tp").astype(jnp.float32)
    stat = jnp.mean(gain_float * whole_grad * act_float, axis=1, keepdims=True) * inv_rms
    grad_slice = lax.dynamic_slice_in_dim(
        whole_grad, lax.axis_index("tp") * own_width, own_width, 1
    )
    grad_scaled = own_gain * grad_slice
    grad_input = (inv_rms * (grad_scaled - own_scaled * stat)).astype(jnp.bfloat16)
    row_share = width // lax.axis_size("seq")
    product = lax.dot_general(
        normed, grad_pre, (((0,), (0,)), ((), ())), preferred_element_type=jnp.float32
    )
    grad_proj = lax.psum_scatter(
        product.reshape(lax.axis_size("seq") * row_share, 3, local_ch).astype(jnp.bfloat16),
        "seq",
        scatter_dimension=0,
        tiled=True,
    )
    return (mixer_out, grad_input, grad_proj)


def solution(mesh):
    return jax.shard_map(
        per_device,
        mesh=mesh,
        in_specs=(
            P("seq", "tp"),
            P("tp"),
            P(None, None, "tp"),
            P(None, None, "tp"),
            P("tp", None),
            P("seq", "tp"),
        ),
        out_specs=(P("seq", "tp"), P("seq", "tp"), P("seq", None, "tp")),
        check_vma=False,
    )
```

profile of v0, /device:TPU:1, one launch (start us, length us, event | category | flops | bytes accessed | tf_op | source)
XLA Modules:
  0.0 847.9 jit_solution(10637052879910510053)
XLA Ops:
  7.2 0.7 all-gather.3.cloned.1.call-update
  7.9 0.0 all-reduce.2.cloned.1.call-start
  7.9 0.7 reshape.189
  8.6 21.9 %all-gather = bf16[16,1,512]{2,1,0:T(2,128)(2,1)S(1)} all-gather(bf16[1,1,512]{2,1,0:T(2,128)(2,1)S(1)} %reshape.189), channel_id=1, replica_groups=mesh['seq'=8,'tp'=16] {'tp'}, dimensions={0}, use_global_device_ids=true | all-gather | bytes 17408 | tf_op jit(solution)/shard_map/all_gather | solution.py:56
  30.5 16.7 %copy.82 = bf16[8192,3,256]{0,2,1:T(8,128)(2,1)} copy(bf16[8192,3,256]{2,0,1:T(8,128)(2,1)} %param.8) | data formatting | bytes 25165824 | tf_op args[2]
  47.3 0.1 copy.88
  47.4 0.1 compare_select_fusion.2
  47.5 0.5 reshape.173
  47.9 0.1 pad_clamp_fusion.1
  48.0 179.6 %gather_fusion = f32[98048,16]{1,0:T(8,128)} fusion(f32[16,128]{0,1:T(8,128)S(1)} %copy.88, s32[98304]{0:T(1024)S(1)} %pad_clamp_fusion.1), kind=kCustom, calls=%fused_computation | custom fusion | bytes 12942336 | tf_op jit(solution)/shard_map/jit(_take)/gather | solution.py:42
  227.6 27.7 %copy.89 = f32[98048,16]{0,1:T(8,128)} copy(f32[98048,16]{1,0:T(8,128)} %gather_fusion) | data formatting | bytes 12550144 | tf_op jit(solution)/shard_map/jit(_take)/gather | solution.py:42
  255.3 10.9 %reshape.176 = f32[256,383,16]{1,0,2:T(8,128)} reshape(f32[98048,16]{0,1:T(8,128)} %copy.89) | data formatting | bytes 12550144 | tf_op jit(solution)/shard_map/jit(_take)/gather | solution.py:42
  266.2 0.1 copy.90
  266.3 0.2 compare_select_fusion
  266.5 0.5 reshape.181
  267.0 0.1 pad_clamp_fusion
  267.0 182.5 %gather_fusion.1 = f32[99330,16]{1,0:T(8,128)} fusion(f32[16,128]{0,1:T(8,128)S(1)} %copy.88, s32[100352]{0:T(1024)S(1)} %pad_clamp_fusion), kind=kCustom, calls=%fused_computation.1 | custom fusion | bytes 13111560 | tf_op jit(solution)/shard_map/jit(_take)/gather | solution.py:42
  449.5 28.0 %copy.96 = f32[99330,16]{0,1:T(8,128)} copy(f32[99330,16]{1,0:T(8,128)} %gather_fusion.1) | data formatting | bytes 12714240 | tf_op jit(solution)/shard_map/jit(_take)/gather | solution.py:42
  477.5 15.4 %reshape.184 = f32[258,385,16]{1,0,2:T(8,128)} reshape(f32[99330,16]{0,1:T(8,128)} %copy.96) | data formatting | bytes 12714240 | tf_op jit(solution)/shard_map/jit(_take)/gather | solution.py:42
  492.9 0.2 fusion.39
  493.2 3.1 fusion.5
  496.3 9.4 %convolution_convert_fusion.1 = bf16[256,768]{1,0:T(8,128)(2,1)S(1)} fusion(bf16[8192,768]{0,1:T(8,128)(2,1)} %bitcast.82, bf16[256,8192]{1,0:T(8,128)(2,1)} %all-gather.3.cloned.1.call-done, f32[8192]{0:T(1024)S(1)} %bitcast.95, f32[256]{0:T(256)S(1)} %add_rsqrt_fusion), kind=kOutput, calls=%fused_computation.31 | convolution fusion | flops 3229810688 | bytes 17204224 | tf_op jit(solution)/shard_map/dot_general | solution.py:69
  505.8 0.2 copy.83
  505.9 0.1 slice.157
  506.1 0.1 slice.158
  506.2 0.1 copy.85
  506.3 0.1 copy.84
  506.4 3.1 collective-permute-start
  509.6 2.8 collective-permute-done
  512.4 0.1 copy.103
  512.6 0.7 add_convert_fusion.1
  513.3 0.1 multiply_convert_fusion.1
  513.3 0.1 slice.172
  513.5 0.1 copy.86
  513.6 6.4 fusion.9
  520.1 0.3 fusion.43
  520.4 0.1 fusion.42
  520.5 0.1 copy.91
  520.6 0.1 copy.92
  520.8 0.1 pad_maximum_fusion.7
  520.9 1.3 collective-permute-start.1
  522.2 0.4 fusion.28
  522.6 0.1 slice.176
  522.7 5.1 collective-permute-done.1
  527.8 0.1 slice.173
  527.9 0.1 copy.93
  528.1 0.1 copy.105
  528.3 0.2 copy.106
  528.5 8.0 fusion.1
  536.4 0.1 fusion.33
  536.5 0.1 pad_maximum_fusion
  536.7 0.6 add_convert_fusion
  537.3 14.4 %fusion = bf16[256,8192]{1,0:T(8,128)(2,1)} fusion(bf16[256,3,256]{0,2,1:T(8,128)(2,1)S(1)} %add_convert_fusion, bf16[8192,3,256]{2,0,1:T(8,128)(2,1)} %param.8), kind=kOutput, calls=%fused_computation.7 | convolution fusion | flops 3223322624 | bytes 17170432 | tf_op jit(solution)/shard_map/dot_general | solution.py:115
  551.7 0.3 reduce-scatter.2.cloned.1.call-start
  552.0 10.4 %convolution_convert_fusion = bf16[8192,3,256]{2,0,1:T(8,128)(2,1)} fusion(bf16[256,8192]{1,0:T(8,128)(2,1)} %all-gather.3.cloned.1.call-done, f32[8192]{0:T(1024)S(1)} %bitcast.96, f32[256]{0:T(256)S(1)} %add_rsqrt_fusion, bf16[256,3,256]{0,2,1:T(8,128)(2,1)S(1)} %add_convert_fusion), kind=kOutput, calls=%fused_computation.2 | convolution fusion | flops 3235905536 | bytes 17204224 | tf_op jit(solution)/shard_map/dot_general | solution.py:130
  562.5 0.7 copy-done.6
  563.1 0.8 copy.100
  563.9 120.6 %all-reduce.2.cloned.1.call-done = bf16[256,8192]{1,0:T(8,128)(2,1)} async-done(((bf16[256,8192]{1,0:T(8,128)(2,1)}), bf16[256,8192]{1,0:T(8,128)(2,1)}) %all-reduce.2.cloned.1.call-update) | async-done | bytes 4194320 | tf_op jit(solution)/shard_map/psum | solution.py:122
  684.5 3.3 convert_element_type.148
  687.8 0.1 copy-done
  687.9 1.3 copy-done.1
  689.2 1.7 fusion.8
  690.9 0.9 multiply_convert_fusion
  691.8 149.6 %reduce-scatter.2.cloned.1.call-done = bf16[1024,3,256]{2,0,1:T(8,128)(2,1)} async-done(((bf16[8192,3,256]{2,0,1:T(8,128)(2,1)}), bf16[1024,3,256]{2,0,1:T(8,128)(2,1)}) %reduce-scatter.2.cloned.1.call-update) | async-done | bytes 1572880 | tf_op jit(solution)/shard_map/reduce_scatter | solution.py:133
  (36 shorter events, 0.5 us)
Async XLA Ops:
  7.2 486.0 %all-gather.3.cloned.1.call-start = ((), (), s32[]{:S(2)}) async-start(), calls=%async_computation.1 | async-start | bytes 4456448 | tf_op jit(solution)/shard_map/all_gather | solution.py:55
  7.9 676.6 %all-reduce.2.cloned.1.call-start = ((), (), s32[]{:S(2)}) async-start(), calls=%async_computation.2 | async-start | bytes 8388608 | tf_op jit(solution)/shard_map/psum | solution.py:122
  30.5 16.8 %copy-start.5 = (f32[16,128]{1,0:T(8,128)S(1)}, f32[16,128]{1,0:T(8,128)}, u32[]{:S(2)}) copy-start(f32[16,128]{1,0:T(8,128)} %param.10) | copy-start | bytes 24580
  255.3 10.9 %copy-start.3 = (bf16[256,256]{1,0:T(8,128)(2,1)S(1)}, bf16[256,256]{1,0:T(8,128)(2,1)}, u32[]{:S(2)}) copy-start(bf16[256,256]{1,0:T(8,128)(2,1)} %param.11) | copy-start | bytes 393220
  477.5 15.6 %copy-start.4 = (f32[3,3,256]{2,1,0:T(4,128)S(1)}, f32[3,3,256]{2,1,0:T(4,128)}, u32[]{:S(2)}) copy-start(f32[3,3,256]{2,1,0:T(4,128)} %param.9) | copy-start | bytes 27652
  506.4 6.0 collective-permute-start
  520.9 6.9 collective-permute-start.1
  551.7 289.7 %reduce-scatter.2.cloned.1.call-start = ((), (), s32[]{:S(2)}) async-start(), calls=%async_computation.3 | async-start | bytes 14155776 | tf_op jit(solution)/shard_map/reduce_scatter | solution.py:133
  562.4 0.7 copy-start.6
  563.9 127.0 %copy-start.2 = (bf16[256,512]{1,0:T(8,128)(2,1)S(1)}, bf16[256,512]{1,0:T(8,128)(2,1)}, u32[]{:S(2)}) copy-start(bf16[256,512]{1,0:T(8,128)(2,1)} %param.6) | copy-start | bytes 786436
  684.5 3.4 copy-start
  684.5 4.7 copy-start.1
Sparse Core Ops, SparseCore 0:
  9.7 40.9 all-gather.2
  551.8 132.6 all-reduce.1
  689.0 152.3 reduce-scatter.1
where the time goes:
time: 849 us; the launch traced here: 848 us
  local copies, waits for them, and re-layouts  468 us (55%)
  waiting for transfers between devices  279 us (33%)
  matrix products  48.6 us (6%)
  blocking collectives  21.9 us (3%)
  between operations  14.1 us (2%)
  other arithmetic  12.1 us (1%)
    gather x6, local copies, waits for them, and re-layouts, band_matrix(): picked = jnp.take(tap_rows, jnp.clip(offsets, 0, LM - 1), axis=1)  444 us
    reduce_scatter x1, waiting for transfers between devices, per_device(): lax.psum_scatter(product.reshape(lax.axis_size('seq') * row_share, 3, loc...  150 us
    psum x1, waiting for transfers between devices, per_device(): lax.psum(partial_grad.astype(jnp.bfloat16), 'tp').astype(jnp.float32)  121 us
    all_gather x1, blocking collectives, per_device(): lax.all_gather(norm_gain, 'tp', axis=0, tiled=True)  21.9 us
    unnamed x22, local copies, waits for them, and re-layouts  20.8 us
  transfers between devices with their start and end apart: 5, of which 4 were waited for; matrix products, arithmetic and copies ran while one was open for 57% of the time, Pallas kernels for 0%

commit v1 on v0

v1 whole, which is shorter than its diff:
```python
import functools

import jax
import jax.numpy as jnp
from jax import lax
from jax.experimental import pallas as pl
from jax.experimental.pallas import tpu as pltpu
from jax.sharding import PartitionSpec as P

GROUP = 16
LM = 128
BLK = 128
EPS = 1e-06
F32 = jnp.float32
BF16 = jnp.bfloat16
MESH = pl.DeviceIdType.MESH


def build_bands(rows_ref, band_ref):
    def one(g, carry):
        row = jnp.broadcast_to(rows_ref[pl.ds(g, 1), :], (BLK, 2 * BLK))
        band_ref[g] = pltpu.roll(row, 0, 1, stride=1, stride_axis=0).astype(BF16)
        return carry

    lax.fori_loop(0, rows_ref.shape[0], one, 0)


def apply_band(band_ref, first, source_ref, row0):
    lane = lax.broadcasted_iota(jnp.int32, (BLK, 128), 1) // GROUP
    halves = source_ref.shape[1] // 128

    def one(g, totals):
        new = []
        for h in range(halves):
            part = jnp.dot(
                band_ref[first + h * 8 + g],
                source_ref[row0 : row0 + 2 * BLK, h * 128 : h * 128 + 128],
                preferred_element_type=F32,
            )
            new.append(jnp.where(lane == g, part, totals[h]))
        return tuple(new)

    totals = lax.fori_loop(0, 8, one, tuple(jnp.zeros((BLK, 128), F32) for _ in range(halves)))
    return jnp.concatenate(totals, 1)


def mixer(pre, cot, taps, band, mix, gp, ext, feat, gext, gfext, gft, ptail, ghead, gtail, send, recv):
    tok, ch = pre.shape[1], pre.shape[2]
    n = lax.axis_size("seq")
    me = lax.axis_index("seq")
    after, before = lax.rem(me + 1, n), lax.rem(me + n - 1, n)
    first, last = me == 0, me == n - 1
    groups = ch // GROUP

    def remote(src, dst, index, to):
        return pltpu.make_async_remote_copy(
            src_ref=src, dst_ref=dst, send_sem=send.at[index], recv_sem=recv.at[index],
            device_id={"seq": to}, device_id_type=MESH,
        )

    tail_copy = remote(pre.at[:, pl.ds(tok - 16, 16), :], ptail, 0, after)
    tail_copy.start()
    for j in range(3):
        ext[j, 8 : 8 + tok, :] = pre[j].astype(F32)

    def short(j, lo, hi):
        total = taps[0, j : j + 1, :] * ext[j, 8 + lo : 8 + hi, :]
        total += taps[1, j : j + 1, :] * ext[j, 7 + lo : 7 + hi, :]
        total += taps[2, j : j + 1, :] * ext[j, 6 + lo : 6 + hi, :]
        return total.astype(BF16)

    def gate(lo, hi):
        k, v = short(1, lo, hi), short(2, lo, hi)
        feat[1, lo:hi, :] = k
        feat[2, lo:hi, :] = v
        gext[BLK + lo : BLK + hi, :] = (k.astype(F32) * v.astype(F32)).astype(BF16)

    gate(tok - BLK, tok)
    gated_copy = remote(gext.at[pl.ds(tok, BLK), :], gext.at[pl.ds(0, BLK), :], 1, after)
    gated_copy.start()

    tail_copy.wait_recv()
    for j in range(3):
        ext[j, 0:8, :] = jnp.where(first, 0.0, ptail[j].astype(F32)[8:16])
    q = short(0, 0, tok)
    feat[0] = q
    grad_out = cot[...].astype(F32)
    gfext[0:tok, :] = (grad_out * q.astype(F32)).astype(BF16)
    filt_copy = remote(gfext.at[pl.ds(0, BLK), :], gtail, 2, before)
    filt_copy.start()
    gate(0, tok - BLK)

    def grad_kv(lo):
        gg = apply_band(band, groups, gfext, lo)
        gft[1, lo : lo + BLK, :] = (gg * feat[2, lo : lo + BLK, :].astype(F32)).astype(BF16).astype(F32)
        gft[2, lo : lo + BLK, :] = (gg * feat[1, lo : lo + BLK, :].astype(F32)).astype(BF16).astype(F32)

    def forward(lo):
        filt = apply_band(band, 0, gext, lo)
        mix[lo : lo + BLK, :] = (feat[0, lo : lo + BLK, :].astype(F32) * filt).astype(BF16)
        gft[0, lo : lo + BLK, :] = (cot[lo : lo + BLK, :].astype(F32) * filt).astype(BF16).astype(F32)

    grad_kv(0)
    gated_copy.wait_recv()

    @pl.when(first)
    def _():
        gext[0:BLK, :] = jnp.zeros((BLK, ch), BF16)

    forward(0)
    for j in range(3):
        ghead[0, j] = gft[j, 0:16, :].astype(BF16)
    head_copy = remote(ghead.at[0], ghead.at[1], 3, before)
    head_copy.start()
    forward(BLK)
    filt_copy.wait_recv()
    gfext[tok : tok + BLK, :] = jnp.where(last, 0.0, gtail[...].astype(F32)).astype(BF16)
    grad_kv(BLK)
    head_copy.wait_recv()
    for j in range(3):
        gft[j, tok : tok + 8, :] = jnp.where(last, 0.0, ghead[1, j].astype(F32)[0:8])
    for j in range(3):
        total = taps[0, j : j + 1, :] * gft[j, 0:tok, :]
        total += taps[1, j : j + 1, :] * gft[j, 1 : tok + 1, :]
        total += taps[2, j : j + 1, :] * gft[j, 2 : tok + 2, :]
        gp[j] = total.astype(BF16)
    for copy in (tail_copy, gated_copy, filt_copy, head_copy):
        copy.wait_send()


def mixer_scratch(tok, ch):
    return [
        pltpu.VMEM((2 * ch // GROUP, BLK, 2 * BLK), BF16),
        pltpu.VMEM((3, tok + 8, ch), F32),
        pltpu.VMEM((3, tok, ch), BF16),
        pltpu.VMEM((tok + BLK, ch), BF16),
        pltpu.VMEM((tok + BLK, ch), BF16),
        pltpu.VMEM((3, tok + 8, ch), F32),
        pltpu.VMEM((3, 16, ch), BF16),
        pltpu.VMEM((2, 3, 16, ch), BF16),
        pltpu.VMEM((BLK, ch), BF16),
        pltpu.SemaphoreType.DMA((4,)),
        pltpu.SemaphoreType.DMA((4,)),
    ]


def mixer_kernel(pre, cot, taps, rows, mix, gp, band, *scratch):
    n = lax.axis_size("seq")
    me = lax.axis_index("seq")
    barrier = pltpu.get_barrier_semaphore()
    for to in (lax.rem(me + 1, n), lax.rem(me + n - 1, n)):
        pl.semaphore_signal(barrier, inc=1, device_id={"seq": to}, device_id_type=MESH)
    build_bands(rows, band)
    pl.semaphore_wait(barrier, 2)
    mixer(pre, cot, taps, band, mix, gp, *scratch)


def band_rows(medium_taps):
    zero = jnp.zeros_like(medium_taps)
    forward = jnp.concatenate([zero[:, :1], medium_taps[:, ::-1], zero[:, 1:]], 1)
    backward = jnp.concatenate([medium_taps, zero], 1)
    return jnp.concatenate([forward, backward], 0)


def per_device(activations, norm_gain, in_proj, short_taps, medium_taps, cotangent):
    tok, own_width = activations.shape
    ch = in_proj.shape[2]
    act_full = lax.all_gather(activations, "tp", axis=1, tiled=True)
    gain_full = lax.all_gather(norm_gain, "tp", axis=0, tiled=True)
    width = act_full.shape[1]
    act_cols = lax.all_to_all(act_full, "seq", split_axis=1, concat_axis=0, tiled=True)
    act_float = act_full.astype(F32)
    inv_rms = lax.rsqrt(jnp.mean(act_float * act_float, axis=1, keepdims=True) + EPS)
    normed = (act_float * inv_rms * gain_full.astype(F32)).astype(BF16)
    weight = jnp.transpose(in_proj, (1, 0, 2))
    pre = jnp.einsum("td,jdc->jtc", normed, weight, preferred_element_type=F32).astype(BF16)
    vmem = pl.BlockSpec(memory_space=pltpu.VMEM)
    mix, gp = pl.pallas_call(
        mixer_kernel,
        out_shape=(
            jax.ShapeDtypeStruct((tok, ch), BF16),
            jax.ShapeDtypeStruct((3, tok, ch), BF16),
        ),
        in_specs=[vmem] * 4,
        out_specs=(vmem, vmem),
        scratch_shapes=mixer_scratch(tok, ch),
        compiler_params=pltpu.CompilerParams(
            collective_id=0, has_side_effects=True, vmem_limit_bytes=40 * 2**20
        ),
    )(pre, cotangent, short_taps, band_rows(medium_taps))
    stat = lax.psum(jnp.sum(gp.astype(F32) * pre.astype(F32), axis=(0, 2)), "tp")[:, None] / width
    sent = (gp.astype(F32) * inv_rms[None]).astype(BF16)
    gp_all = lax.all_gather(sent, "seq", axis=1, tiled=True)
    partial = jnp.einsum("jtc,jdc->td", gp, weight, preferred_element_type=F32).astype(BF16)
    grad_slice = lax.psum_scatter(partial, "tp", scatter_dimension=1, tiled=True).astype(F32)
    own_scaled = activations.astype(F32) * inv_rms
    grad_input = (inv_rms * (norm_gain.astype(F32) * grad_slice - own_scaled * stat)).astype(BF16)
    product = jnp.einsum("td,jtc->jdc", act_cols, gp_all, preferred_element_type=F32)
    share = width // lax.axis_size("seq")
    own_gain = lax.dynamic_slice_in_dim(gain_full, lax.axis_index("seq") * share, share, 0).astype(F32)
    grad_proj = (product * own_gain[None, :, None]).astype(BF16).transpose(1, 0, 2)
    return mix, grad_input, grad_proj


def solution(mesh):
    return jax.shard_map(
        per_device,
        mesh=mesh,
        in_specs=(
            P("seq", "tp"), P("tp"), P(None, None, "tp"), P(None, None, "tp"), P("tp", None), P("seq", "tp"),
        ),
        out_specs=(P("seq", "tp"), P("seq", "tp"), P("seq", None, "tp")),
        check_vma=False,
    )
```

time: 849 us -> 252 us (0.30)
  local copies, waits for them, and re-layouts: 468 us -> 8.67 us
  waiting for transfers between devices: 279 us -> 84.8 us
  blocking collectives: 21.9 us -> 87 us
  matrix products: 48.6 us -> 27.5 us
  Pallas kernels: 0 us -> 15.3 us
    gather x6 -> x0, local copies, waits for them, and re-layouts: 444 us -> none  [band_matrix(): picked = jnp.take(tap_rows, jnp.clip(offsets, 0, LM - 1), axis=1)]
    psum x1 -> x0, waiting for transfers between devices: 121 us -> none  [per_device(): lax.psum(partial_grad.astype(jnp.bfloat16), 'tp').astype(jnp.float32)]
    reduce_scatter x1, waiting for transfers between devices: 150 us -> 54.9 us  [per_device(): lax.psum_scatter(partial, 'tp', scatter_dimension=1, tiled=True).astype(F32)]
    psum x0 -> x1, blocking collectives: none -> 65.2 us  [per_device(): lax.psum(jnp.sum(gp.astype(F32) * pre.astype(F32), axis=(0, 2)), 'tp')]
    all_gather x1 -> x2, waiting for transfers between devices: 0.02 us -> 29.1 us  [the longest x1 18.5 us: per_device(): act_full = lax.all_gather(activations, 'tp', axis=1, tiled=True)]
    dot_general x5 -> x3, matrix products: 48.6 us -> 27.5 us  [the longest x1 14.2 us: per_device(): jnp.einsum('jtc,jdc->td', gp, weight, preferred_element_type=F32)]
    unnamed x22 -> x14, local copies, waits for them, and re-layouts: 20.8 us -> 3.12 us
    pallas_call x0 -> x1, Pallas kernels: none -> 15.3 us  [per_device(): pl.pallas_call(mixer_kernel, out_shape=(jax.ShapeDtypeStruct((tok, ch), B...]
  transfers between devices with their start and end apart: 5 -> 4, of which waited for: 4 -> 3; matrix products, arithmetic and copies ran while one was open for 57% -> 12% of each run, Pallas kernels for 0% -> 0%
where the time goes in v1:
time: 252 us; the launch traced here: 249 us
  blocking collectives  87 us (35%)
  waiting for transfers between devices  84.8 us (34%)
  matrix products  27.5 us (11%)
  Pallas kernels  15.3 us (6%)
  between operations  13.8 us (5%)
  local copies, waits for them, and re-layouts  8.67 us (3%)
  other arithmetic  7.01 us (3%)
  starting transfers between devices  4.94 us (2%)
    psum x1, blocking collectives, per_device(): lax.psum(jnp.sum(gp.astype(F32) * pre.astype(F32), axis=(0, 2)), 'tp')  65.2 us
    reduce_scatter x1, waiting for transfers between devices, per_device(): lax.psum_scatter(partial, 'tp', scatter_dimension=1, tiled=True).astype(F32)  54.9 us
    all_gather x1, blocking collectives, per_device(): gain_full = lax.all_gather(norm_gain, 'tp', axis=0, tiled=True)  21.9 us
    all_gather x1, waiting for transfers between devices, per_device(): act_full = lax.all_gather(activations, 'tp', axis=1, tiled=True)  18.5 us
    pallas_call x1, Pallas kernels, per_device(): pl.pallas_call(mixer_kernel, out_shape=(jax.ShapeDtypeStruct((tok, ch), B...  15.3 us
    dot_general x1, matrix products, per_device(): jnp.einsum('jtc,jdc->td', gp, weight, preferred_element_type=F32)  14.2 us
    all_gather x1, waiting for transfers between devices, per_device(): gp_all = lax.all_gather(sent, 'seq', axis=1, tiled=True)  10.6 us
    dot_general x1, matrix products, per_device(): jnp.einsum('td,jdc->jtc', normed, weight, preferred_element_type=F32)  6.7 us
  transfers between devices with their start and end apart: 4, of which 3 were waited for; matrix products, arithmetic and copies ran while one was open for 12% of the time, Pallas kernels for 0%

profile of v1, /device:TPU:1, one launch (start us, length us, event | category | flops | bytes accessed | tf_op | source)
XLA Modules:
  0.0 249.1 jit_solution(17818129237351168556)
XLA Ops:
  7.2 0.0 all-gather.4.cloned.1.call-start
  7.2 0.7 all-gather.4.cloned.1.call-update
  7.9 0.0 all-gather.6.cloned.1.call-start
  7.9 0.7 reshape.27
  8.6 21.9 %all-gather = bf16[16,1,512]{2,1,0:T(2,128)(2,1)S(1)} all-gather(bf16[1,1,512]{2,1,0:T(2,128)(2,1)S(1)} %reshape.27), channel_id=1, replica_groups=mesh['seq'=8,'tp'=16] {'tp'}, dimensions={0}, use_global_device_ids=true | all-gather | bytes 17408 | tf_op jit(solution)/shard_map/all_gather | solution.py:169
  30.5 0.1 reduce
  30.6 0.8 rev.3
  31.4 0.8 select_maximum_fusion.rows
  32.2 18.5 %all-gather.4.cloned.1.call-done = bf16[256,8192]{1,0:T(8,128)(2,1)} async-done(((bf16[256,512]{1,0:T(8,128)(2,1)}), bf16[256,8192]{1,0:T(8,128)(2,1)}) %all-gather.4.cloned.1.call-update) | async-done | bytes 4194320 | tf_op jit(solution)/shard_map/all_gather | solution.py:168
  50.7 0.0 copy-start.2
  50.7 3.3 %fusion.10 = f32[256]{0:T(256)S(1)} fusion(bf16[256,8192]{1,0:T(8,128)(2,1)} %all-gather.4.cloned.1.call-done), kind=kLoop, calls=%fused_computation.8 | loop fusion | flops 6291200 | bytes 4195328 | tf_op jit(solution)/shard_map/reduce_sum | solution.py:173
  54.0 0.2 copy-done.2
  54.1 0.0 copy-start
  54.1 0.0 copy-start.1
  54.1 6.7 %fusion.23.pre = bf16[3,256,256]{2,1,0:T(8,128)(2,1)S(1)} fusion(bf16[8192,3,256]{2,0,1:T(8,128)(2,1)} %param.8, bf16[256,8192]{1,0:T(8,128)(2,1)S(1)} %copy-done.2, f32[8192]{0:T(1024)S(1)} %convert_element_type.50, f32[256]{0:T(256)S(1)} %add_rsqrt_fusion), kind=kOutput, calls=%fused_computation.18 | convolution fusion | flops 3229810688 | bytes 17204224 | tf_op jit(solution)/shard_map/td,jdc->jtc/dot_general | solution.py:176
  60.9 0.0 copy-done
  60.9 0.0 copy-done.1
  60.9 15.3 %shard_map.85 = (bf16[256,256]{1,0:T(8,128)(2,1)S(1)}, bf16[3,256,256]{2,1,0:T(8,128)(2,1)S(1)}) custom-call(bf16[3,256,256]{2,1,0:T(8,128)(2,1)S(1)} %fusion.23.pre, bf16[256,256]{1,0:T(8,128)(2,1)S(1)} %copy-done, f32[3,3,256]{2,1,0:T(4,128)S(1)} %copy-done.1, f32[32,256]{1,0:T(8,128)S(1)} %select_maximum_fusion.rows), custom_call_target="tpu_custom_call" | custom-call | tf_op jit(solution)/shard_map/pallas_call | solution.py:178
  76.2 1.0 fusion.29
  77.3 0.0 all-gather.6.cloned.1.call-update
  77.3 0.0 reduce-scatter.2.cloned.1.call-start
  77.3 14.2 %fusion.7 = bf16[256,8192]{1,0:T(8,128)(2,1)} fusion(bf16[3,256,256]{2,1,0:T(8,128)(2,1)S(1)} %get-tuple-element.6, bf16[8192,3,256]{2,0,1:T(8,128)(2,1)} %param.8), kind=kOutput, calls=%fused_computation.7 | convolution fusion | flops 3223322624 | bytes 17170432 | tf_op jit(solution)/shard_map/jtc,jdc->td/dot_general | solution.py:194
  91.5 0.0 reduce-scatter.2.cloned.1.call-update
  91.5 4.8 %copy.30 = bf16[32,8,8,1024]{3,2,0,1:T(8,128)(2,1)} copy(bf16[32,8,8,1024]{3,2,1,0:T(8,128)(2,1)} %bitcast.42) | data formatting | bytes 8388608 | tf_op jit(solution)/shard_map/all_to_all | solution.py:171
  96.3 0.0 copy-start.4
  96.3 4.8 %all-to-all-start = ((bf16[256,8,1024]{2,0,1:T(8,128)(2,1)}), bf16[256,8,1024]{2,0,1:T(8,128)(2,1)}, u32[]{:S(2)}, u32[]{:S(2)}) async-start(bf16[256,8,1024]{2,0,1:T(8,128)(2,1)} %bitcast.43), calls=%async_computation.1 | async-start | bytes 8388608 | tf_op jit(solution)/shard_map/all_to_all | solution.py:171
  101.2 0.0 copy-done.4
  101.2 65.2 %psum.7 = f32[256]{0:T(256)S(1)} all-reduce(f32[256]{0:T(256)S(1)} %get-tuple-element.17), channel_id=1, replica_groups=mesh['seq'=8,'tp'=16] {'tp'}, use_global_device_ids=true, to_apply=%region_3.0 | all-reduce | flops 256 | bytes 2048 | tf_op jit(solution)/shard_map/psum | solution.py:191
  166.4 0.0 all-to-all-done
  166.4 10.6 %all-gather.6.cloned.1.call-done = bf16[3,2048,256]{2,1,0:T(8,128)(2,1)} async-done(((bf16[3,256,256]{2,1,0:T(8,128)(2,1)}), bf16[3,2048,256]{2,1,0:T(8,128)(2,1)}) %all-gather.6.cloned.1.call-update) | async-done | bytes 3145744 | tf_op jit(solution)/shard_map/all_gather | solution.py:193
  177.0 0.0 copy-start.3
  177.0 6.6 %fusion.17 = bf16[1024,3,256]{0,2,1:T(8,128)(2,1)S(1)} fusion(f32[1024]{0:T(1024)S(1)} %dynamic-slice_convert_fusion, bf16[3,2048,256]{2,1,0:T(8,128)(2,1)} %all-gather.6.cloned.1.call-done, bf16[2048,1024,1]{1,0,2:T(8,128)(2,1)} %bitcast.6), kind=kOutput, calls=%fused_computation.16 | convolution fusion | flops 3222798336 | bytes 8916992 | tf_op jit(solution)/shard_map/td,jtc->jdc/dot_general | solution.py:198
  183.6 1.6 copy.23
  185.2 54.9 %reduce-scatter.2.cloned.1.call-done = bf16[256,512]{1,0:T(8,128)(2,1)} async-done(((bf16[256,8192]{1,0:T(8,128)(2,1)}), bf16[256,512]{1,0:T(8,128)(2,1)}) %reduce-scatter.2.cloned.1.call-update) | async-done | bytes 262160 | tf_op jit(solution)/shard_map/reduce_scatter | solution.py:195
  240.1 0.0 copy-done.3
  240.1 1.8 multiply_convert_fusion.1
  241.9 0.7 copy.32
  (8 shorter events, 0.0 us)
Async XLA Ops:
  7.2 43.5 %all-gather.4.cloned.1.call-start = ((), (), s32[]{:S(2)}) async-start(), calls=%async_computation.2 | async-start | bytes 4456448 | tf_op jit(solution)/shard_map/all_gather | solution.py:168
  7.9 169.1 %all-gather.6.cloned.1.call-start = ((), (), s32[]{:S(2)}) async-start(), calls=%async_computation.4 | async-start | bytes 3538944 | tf_op jit(solution)/shard_map/all_gather | solution.py:193
  50.7 3.4 %copy-start.2 = (bf16[256,8192]{1,0:T(8,128)(2,1)S(1)}, bf16[256,8192]{1,0:T(8,128)(2,1)}, u32[]{:S(2)}) copy-start(bf16[256,8192]{1,0:T(8,128)(2,1)} %all-gather.4.cloned.1.call-done) | copy-start | bytes 12582916
  54.1 6.7 %copy-start = (bf16[256,256]{1,0:T(8,128)(2,1)S(1)}, bf16[256,256]{1,0:T(8,128)(2,1)}, u32[]{:S(2)}) copy-start(bf16[256,256]{1,0:T(8,128)(2,1)} %cot.1) | copy-start | bytes 393220
  54.1 6.7 %copy-start.1 = (f32[3,3,256]{2,1,0:T(4,128)S(1)}, f32[3,3,256]{2,1,0:T(4,128)}, u32[]{:S(2)}) copy-start(f32[3,3,256]{2,1,0:T(4,128)} %taps.1) | copy-start | bytes 27652
  77.3 162.8 %reduce-scatter.2.cloned.1.call-start = ((), (), s32[]{:S(2)}) async-start(), calls=%async_computation.3 | async-start | bytes 4456448 | tf_op jit(solution)/shard_map/reduce_scatter | solution.py:195
  96.3 4.8 %copy-start.4 = (bf16[512]{0:T(512)(128)(2,1)S(1)}, bf16[512]{0:T(512)(128)(2,1)}, u32[]{:S(2)}) copy-start(bf16[512]{0:T(512)(128)(2,1)} %param.7) | copy-start | bytes 3076
  96.3 70.0 %all-to-all-start = ((bf16[256,8,1024]{2,0,1:T(8,128)(2,1)}), bf16[256,8,1024]{2,0,1:T(8,128)(2,1)}, u32[]{:S(2)}, u32[]{:S(2)}) async-start(bf16[256,8,1024]{2,0,1:T(8,128)(2,1)} %bitcast.43), calls=%async_computation.1 | async-start | bytes 8388608 | tf_op jit(solution)/shard_map/all_to_all | solution.py:171
  177.0 63.1 %copy-start.3 = (bf16[256,512]{1,0:T(8,128)(2,1)S(1)}, bf16[256,512]{1,0:T(8,128)(2,1)}, u32[]{:S(2)}) copy-start(bf16[256,512]{1,0:T(8,128)(2,1)} %param.6) | copy-start | bytes 786436
Sparse Core Ops, SparseCore 0:
  9.7 40.9 all-gather.3
  77.4 99.5 all-gather.5
  179.4 60.6 reduce-scatter.1

commit v2 on v1

--- a/solution.py
+++ b/solution.py
@@ -144,15 +144,295 @@
     ]
 
 
-def mixer_kernel(pre, cot, taps, rows, mix, gp, band, *scratch):
-    n = lax.axis_size("seq")
-    me = lax.axis_index("seq")
+def whole_kernel(
+    act, gain, weight, cot, taps, rows, mix, grad_in, grad_proj,
+    ag, w, acc, ssq, inv, pre, gp, col, cols_t, gp_all, total, sib_out, sib_in, pair_out, pair_in, part, stats,
+    load_sem, w_sem, ag_sem, fwd_sem, col_sem, colf_sem, gp_sem, sib_sem, pair_sem, stat_sem, statp_sem,
+    band, *halo,
+):
+    n_seq, n_tp = lax.axis_size("seq"), lax.axis_size("tp")
+    tok, own = act.shape
+    ch = pre.shape[2]
+    chips = n_tp // 2
+    s, p = lax.axis_index("seq"), lax.axis_index("tp")
+    q, core = p // 2, lax.rem(p, 2)
+    sib = p + 1 - 2 * core
+    width = n_tp * own
+
+    def remote(src, dst, sems, index, to):
+        return pltpu.make_async_remote_copy(
+            src_ref=src, dst_ref=dst, send_sem=sems.at[0, index], recv_sem=sems.at[1, index],
+            device_id=to, device_id_type=MESH,
+        )
+
+    def tp_peer(k):
+        return lax.rem(q + k, chips) * 2 + core
+
+    def tp_source(k):
+        return lax.rem(q + chips - k, chips)
+
+    def loop(lo, hi, body):
+        def step(i, carry):
+            body(i)
+            return carry
+
+        lax.fori_loop(lo, hi, step, 0)
+
+    def block_rows(index):
+        return pl.ds(pl.multiple_of(index * own, own), own)
+
+    loads = (
+        pltpu.make_async_copy(act, ag.at[p, pl.ds(0, tok), :], load_sem.at[0]),
+        pltpu.make_async_copy(gain, ag.at[p, pl.ds(tok, 16), :], load_sem.at[1]),
+    )
+    for copy in loads:
+        copy.start()
+
+    def w_copy(index):
+        return pltpu.make_async_copy(
+            weight.at[:, block_rows(index), :], w.at[:, block_rows(index), :], w_sem.at[index]
+        )
+
+    loop(0, n_tp, lambda i: w_copy(lax.rem(p + i, n_tp)).start())
+
     barrier = pltpu.get_barrier_semaphore()
-    for to in (lax.rem(me + 1, n), lax.rem(me + n - 1, n)):
-        pl.semaphore_signal(barrier, inc=1, device_id={"seq": to}, device_id_type=MESH)
+
+    def greet(k):
+        pl.semaphore_signal(barrier, inc=1, device_id={"seq": s, "tp": tp_peer(k)}, device_id_type=MESH)
+        to = lax.rem(s + k, n_seq)
+        pl.semaphore_signal(barrier, inc=1, device_id={"seq": to, "tp": p}, device_id_type=MESH)
+
+    loop(1, 8, greet)
+    pl.semaphore_signal(barrier, inc=1, device_id={"seq": s, "tp": sib}, device_id_type=MESH)
+    for copy in loads:
+        copy.wait()
+    pl.semaphore_wait(barrier, 15)
+
+    def ag_copy(k):
+        return remote(ag.at[p], ag.at[p], ag_sem, k, {"tp": tp_peer(k)})
+
+    def ag_in(k):
+        slot = tp_source(k) * 2 + core
+        return remote(ag.at[slot], ag.at[slot], ag_sem, k, {"tp": sib})
+
+    def fwd_copy(k):
+        slot = tp_source(k) * 2 + core
+        return remote(ag.at[slot], ag.at[slot], fwd_sem, k, {"tp": sib})
+
+    def fwd_in(k):
+        slot = tp_source(k) * 2 + 1 - core
+        return remote(ag.at[slot], ag.at[slot], fwd_sem, k, {"tp": sib})
+
+    def col_send(to):
+        return pltpu.make_async_remote_copy(
+            src_ref=ag.at[to * 2 + core, pl.ds(0, tok), :], dst_ref=col.at[s, core],
+            send_sem=col_sem.at[0, to], recv_sem=col_sem.at[1, s],
+            device_id={"seq": to}, device_id_type=MESH,
+        )
+
+    def col_in(source):
+        return pltpu.make_async_remote_copy(
+            src_ref=col.at[source, core], dst_ref=col.at[source, core],
+            send_sem=col_sem.at[0, source], recv_sem=col_sem.at[1, source],
+            device_id={"seq": source}, device_id_type=MESH,
+        )
+
+    loop(1, chips, lambda k: ag_copy(k).start())
     build_bands(rows, band)
-    pl.semaphore_wait(barrier, 2)
-    mixer(pre, cot, taps, band, mix, gp, *scratch)
+
+    acc[...] = jnp.zeros_like(acc)
+    ssq[...] = jnp.zeros_like(ssq)
+
+    def absorb(slot):
+        w_copy(slot).wait()
+        x = ag[slot, 0:tok, :].astype(F32)
+        g = ag[slot, tok : tok + 16, :].astype(F32)[0:1]
+        square = x * x
+        ssq[...] += sum(square[:, i * 128 : i * 128 + 128] for i in range(own // 128))
+        scaled = (x * g).astype(BF16)
+        for j in range(3):
+            acc[j] += jnp.dot(scaled, w[j, block_rows(slot), :], preferred_element_type=F32)
+
+    def gather(k):
+        @pl.when(k > 0)
+        def _():
+            ag_in(k).wait_recv()
+
+        source = tp_source(k)
+        fwd_copy(k).start()
+
+        @pl.when(source != s)
+        def _():
+            col_send(source).start()
+
+        absorb(source * 2 + core)
+        fwd_in(k).wait_recv()
+        absorb(source * 2 + 1 - core)
+
+    loop(0, chips, gather)
+
+    inv[...] = jnp.broadcast_to(
+        lax.rsqrt(jnp.sum(ssq[...], axis=1, keepdims=True) * (1.0 / width) + EPS), inv.shape
+    )
+    for j in range(3):
+        pre[j] = (acc[j] * inv[:, 0:1]).astype(BF16)
+
+    mixer(pre, cot, taps, band, mix, gp, *halo)
+
+    def gp_copy(k):
+        return remote(gp_all.at[s], gp_all.at[s], gp_sem, k, {"seq": lax.rem(s + k, n_seq)})
+
+    def gp_in(k):
+        slot = lax.rem(s + n_seq - k, n_seq)
+        return remote(gp_all.at[slot], gp_all.at[slot], gp_sem, k, {"seq": slot})
+
+    stat = jnp.zeros((tok, ch), F32)
+    for j in range(3):
+        value = gp[j].astype(F32)
+        gp_all[s, j] = (value * inv[:, 0:1]).astype(BF16)
+        stat += value * pre[j].astype(F32)
+    loop(1, n_seq, lambda k: gp_copy(k).start())
+
+    eye = lax.broadcasted_iota(jnp.int32, (128, 128), 0) == lax.broadcasted_iota(jnp.int32, (128, 128), 1)
+
+    stat = jnp.sum(stat, axis=1, keepdims=True)
+    stats[0] = jnp.zeros((8, 128), F32)
+    for h in range(tok // 128):
+        piece = jnp.where(eye, stat[h * 128 : h * 128 + 128], 0.0)
+        stats[0, h : h + 1, :] = jnp.sum(piece, axis=0, keepdims=True)
+    stat_sib = remote(stats.at[0], stats.at[1], statp_sem, 0, {"tp": sib})
+    stat_sib.start()
+
+    def partial(rows_):
+        value = None
+        for j in range(3):
+            term = lax.dot_general(
+                gp[j], w[j, rows_, :], (((1,), (1,)), ((), ())), preferred_element_type=F32
+            )
+            value = term if value is None else value + term
+        return value
+
+    def sib_copy(i):
+        return remote(sib_out.at[i], sib_in.at[i], sib_sem, i, {"tp": sib})
+
+    def pair_copy(i):
+        return remote(pair_out.at[i], pair_in.at[i], pair_sem, i, {"tp": tp_peer(i + 1)})
+
+    def finish(i):
+        sib_copy(i).wait_recv()
+        pair_out[i] = (part[lax.rem(i, 2)] + sib_in[i].astype(F32)).astype(BF16)
+        pair_copy(i).start()
+
+    def reduce(i):
+        chip = lax.rem(q + 1 + i, chips)
+        sib_out[i] = partial(block_rows(chip * 2 + 1 - core)).astype(BF16)
+        sib_copy(i).start()
+        part[lax.rem(i, 2)] = partial(block_rows(chip * 2 + core))
+
+        @pl.when(i > 0)
+        def _():
+            finish(i - 1)
+
+    loop(0, chips, reduce)
+
+    stat_sib.wait_recv()
+    stats[2] = stats[0] + stats[1]
+
+    def stat_copy(k):
+        return remote(stats.at[2], stats.at[2 + k], stat_sem, k, {"tp": tp_peer(k)})
+
+    loop(1, chips, lambda k: stat_copy(k).start())
+
+    def colf_copy(source):
+        return remote(col.at[source, core], col.at[source, core], colf_sem, source, {"tp": sib})
+
+    def colf_in(source):
+        return remote(col.at[source, 1 - core], col.at[source, 1 - core], colf_sem, source, {"tp": sib})
+
+    def seq_source(k):
+        return lax.rem(s + n_seq - k, n_seq)
+
+    def turn(source):
+        for half in range(2):
+            cols_t[source, half * own : half * own + own, :] = col[source, half].T
+
+    def pass_on(k):
+        col_in(seq_source(k)).wait_recv()
+        colf_copy(seq_source(k)).start()
+
+    for half in range(2):
+        col[s, half] = ag[s * 2 + half, 0:tok, :]
+    turn(s)
+    loop(1, n_seq, pass_on)
+
+    def turn_next(k):
+        colf_in(seq_source(k)).wait_recv()
+        turn(seq_source(k))
+
+    loop(1, n_seq, turn_next)
+
+    sib_copy(chips - 1).wait_recv()
+    summed = part[(chips - 1) % 2] + sib_in[chips - 1].astype(F32)
+    part[0] = summed
+
+    def collect(k):
+        pair_copy(k - 1).wait_recv()
+        stat_copy(k).wait_recv()
+        part[0] += pair_in[k - 1].astype(F32)
+
+    loop(1, chips, collect)
+    stat_rows = sum(stats[2 + k] for k in range(chips)) * (1.0 / width)
+    own_gain = ag[p, tok : tok + 16, :].astype(F32)[0:1]
+    for h in range(tok // 128):
+        r = slice(h * 128, h * 128 + 128)
+        stat_col = jnp.sum(jnp.where(eye, stat_rows[h : h + 1, :], 0.0), axis=1, keepdims=True)
+        rms = inv[r, 0:1]
+        scaled = ag[p, r, :].astype(F32) * rms
+        grad_in[r, :] = (rms * (own_gain * part[0, r, :] - scaled * stat_col)).astype(BF16)
+
+    total[...] = jnp.zeros_like(total)
+
+    def product(k):
+        @pl.when(k > 0)
+        def _():
+            gp_in(k).wait_recv()
+
+        source = seq_source(k)
+
+        def piece(c):
+            r = pl.ds(pl.multiple_of(c * 128, 128), 128)
+            left = cols_t[source, r, :]
+            for j in range(3):
+                total[j, r, :] += jnp.dot(left, gp_all[source, j], preferred_element_type=F32)
+
+        loop(0, 2 * own // 128, piece)
+
+    loop(0, n_seq, product)
+    for c in range(2 * own // 128):
+        lane = (c * 128) % own
+        g = ag[s * 2 + c * 128 // own, tok : tok + 16, lane : lane + 128].astype(F32)[0:1]
+        g_col = jnp.sum(jnp.where(eye, g, 0.0), axis=1, keepdims=True)
+        for j in range(3):
+            grad_proj[j, c * 128 : c * 128 + 128, :] = (total[j, c * 128 : c * 128 + 128, :] * g_col).astype(BF16)
+
+    def settle(k):
+        @pl.when(k > 0)
+        def _():
+            ag_copy(k).wait_send()
+            gp_copy(k).wait_send()
+            stat_copy(k).wait_send()
+            pair_copy(k - 1).wait_send()
+
+        fwd_copy(k).wait_send()
+        sib_copy(k).wait_send()
+
+        @pl.when(k != s)
+        def _():
+            col_send(k).wait_send()
+            colf_copy(k).wait_send()
+
+    loop(0, chips, settle)
+    stat_sib.wait_send()
 
 
 def band_rows(medium_taps):
@@ -163,43 +443,56 @@
 
 
 def per_device(activations, norm_gain, in_proj, short_taps, medium_taps, cotangent):
-    tok, own_width = activations.shape
-    ch = in_proj.shape[2]
-    act_full = lax.all_gather(activations, "tp", axis=1, tiled=True)
-    gain_full = lax.all_gather(norm_gain, "tp", axis=0, tiled=True)
-    width = act_full.shape[1]
-    act_cols = lax.all_to_all(act_full, "seq", split_axis=1, concat_axis=0, tiled=True)
-    act_float = act_full.astype(F32)
-    inv_rms = lax.rsqrt(jnp.mean(act_float * act_float, axis=1, keepdims=True) + EPS)
-    normed = (act_float * inv_rms * gain_full.astype(F32)).astype(BF16)
-    weight = jnp.transpose(in_proj, (1, 0, 2))
-    pre = jnp.einsum("td,jdc->jtc", normed, weight, preferred_element_type=F32).astype(BF16)
+    tok, own = activations.shape
+    width, _, ch = in_proj.shape
+    n_seq, n_tp = lax.axis_size("seq"), lax.axis_size("tp")
+    chips = n_tp // 2
     vmem = pl.BlockSpec(memory_space=pltpu.VMEM)
-    mix, gp = pl.pallas_call(
-        mixer_kernel,
+    hbm = pl.BlockSpec(memory_space=pl.ANY)
+    sems = lambda count: pltpu.SemaphoreType.DMA((2, count))
+    mix, grad_in, grad_proj = pl.pallas_call(
+        whole_kernel,
         out_shape=(
             jax.ShapeDtypeStruct((tok, ch), BF16),
-            jax.ShapeDtypeStruct((3, tok, ch), BF16),
+            jax.ShapeDtypeStruct((tok, own), BF16),
+            jax.ShapeDtypeStruct((3, 2 * own, ch), BF16),
         ),
-        in_specs=[vmem] * 4,
-        out_specs=(vmem, vmem),
-        scratch_shapes=mixer_scratch(tok, ch),
+        in_specs=[hbm] * 3 + [vmem] * 3,
+        out_specs=(vmem,) * 3,
+        scratch_shapes=[
+            pltpu.VMEM((n_tp, tok + 16, own), BF16),
+            pltpu.VMEM((3, width, ch), BF16),
+            pltpu.VMEM((3, tok, ch), F32),
+            pltpu.VMEM((tok, 128), F32),
+            pltpu.VMEM((tok, 128), F32),
+            pltpu.VMEM((3, tok, ch), BF16),
+            pltpu.VMEM((3, tok, ch), BF16),
+            pltpu.VMEM((n_seq, 2, tok, own), BF16),
+            pltpu.VMEM((n_seq, 2 * own, tok), BF16),
+            pltpu.VMEM((n_seq, 3, tok, ch), BF16),
+            pltpu.VMEM((3, 2 * own, ch), F32),
+            pltpu.VMEM((chips, tok, own), BF16),
+            pltpu.VMEM((chips, tok, own), BF16),
+            pltpu.VMEM((chips, tok, own), BF16),
+            pltpu.VMEM((chips, tok, own), BF16),
+            pltpu.VMEM((2, tok, own), F32),
+            pltpu.VMEM((2 + chips, 8, 128), F32),
+            pltpu.SemaphoreType.DMA((2,)),
+            pltpu.SemaphoreType.DMA((n_tp,)),
+            sems(chips), sems(chips), sems(n_seq), sems(n_seq), sems(n_seq), sems(chips), sems(chips), sems(chips), sems(1),
+        ] + mixer_scratch(tok, ch),
         compiler_params=pltpu.CompilerParams(
-            collective_id=0, has_side_effects=True, vmem_limit_bytes=40 * 2**20
+            collective_id=0, has_side_effects=True, vmem_limit_bytes=60 * 2**20
         ),
-    )(pre, cotangent, short_taps, band_rows(medium_taps))
-    stat = lax.psum(jnp.sum(gp.astype(F32) * pre.astype(F32), axis=(0, 2)), "tp")[:, None] / width
-    sent = (gp.astype(F32) * inv_rms[None]).astype(BF16)
-    gp_all = lax.all_gather(sent, "seq", axis=1, tiled=True)
-    partial = jnp.einsum("jtc,jdc->td", gp, weight, preferred_element_type=F32).astype(BF16)
-    grad_slice = lax.psum_scatter(partial, "tp", scatter_dimension=1, tiled=True).astype(F32)
-    own_scaled = activations.astype(F32) * inv_rms
-    grad_input = (inv_rms * (norm_gain.astype(F32) * grad_slice - own_scaled * stat)).astype(BF16)
-    product = jnp.einsum("td,jtc->jdc", act_cols, gp_all, preferred_element_type=F32)
-    share = width // lax.axis_size("seq")
-    own_gain = lax.dynamic_slice_in_dim(gain_full, lax.axis_index("seq") * share, share, 0).astype(F32)
-    grad_proj = (product * own_gain[None, :, None]).astype(BF16).transpose(1, 0, 2)
-    return mix, grad_input, grad_proj
+    )(
+        activations,
+        jnp.broadcast_to(norm_gain[None], (16, own)),
+        jnp.transpose(in_proj, (1, 0, 2)),
+        cotangent,
+        short_taps,
+        band_rows(medium_taps),
+    )
+    return mix, grad_in, jnp.transpose(grad_proj, (1, 0, 2))
 
 
 def solution(mesh):

time: 252 us -> 164 us (0.65)
  the two profiles are of different devices: /device:TPU:1 before, /device:TPU:6 now
where the time goes in v2:
time: 164 us
  Pallas kernels  154 us (94%)
  local copies, waits for them, and re-layouts  7.95 us (5%)
    pallas_call x1, Pallas kernels, per_device(): pl.pallas_call(whole_kernel, out_shape=(jax.ShapeDtypeStruct((tok, ch), B...  154 us
    unnamed x3, local copies, waits for them, and re-layouts  5.89 us

profile of v2, /device:TPU:6, one launch (start us, length us, event | category | flops | bytes accessed | tf_op | source)
XLA Modules:
  0.0 164.1 jit_solution(16191490987261408251)
XLA Ops:
  0.6 0.8 rev.3
  1.4 1.4 select_maximum_fusion.rows
  2.8 1.3 broadcast_in_dim.2.gain
  4.1 154.1 %shard_map.85 = (bf16[256,256]{1,0:T(8,128)(2,1)}, bf16[256,512]{1,0:T(8,128)(2,1)}, bf16[3,1024,256]{2,1,0:T(8,128)(2,1)}) custom-call(bf16[256,512]{1,0:T(8,128)(2,1)} %act.1, bf16[16,512]{1,0:T(8,128)(2,1)} %broadcast_in_dim.2.gain, bf16[3,8192,256]{2,1,0:T(8,128)(2,1)} %bitcast.2, bf16[256,256]{1,0:T(8,128)(2,1)} %cot.1, f32[3,3,256]{2,1,0:T(4,128)} %taps.1, ...), custom_call_target="tpu_custom_call" | custom-call | tf_op jit(solution)/shard_map/pallas_call | solution.py:453
  158.2 1.6 copy.12
  159.8 1.7 %copy.13 = bf16[256,512]{1,0:T(8,128)(2,1)} copy(bf16[256,512]{1,0:T(8,128)(2,1)} %get-tuple-element.13) | data formatting | bytes 524288
  161.5 2.7 %copy.14 = bf16[1024,3,256]{2,0,1:T(8,128)(2,1)} copy(bf16[1024,3,256]{2,0,1:T(8,128)(2,1)} %bitcast.3) | data formatting | bytes 3145728
  (2 shorter events, 0.0 us)

commit v3 on v2

--- a/solution.py
+++ b/solution.py
@@ -1,5 +1,3 @@
-import functools
-
 import jax
 import jax.numpy as jnp
 from jax import lax
@@ -16,13 +14,19 @@
 MESH = pl.DeviceIdType.MESH
 
 
-def build_bands(rows_ref, band_ref):
+def build_bands(taps_ref, band_ref):
+    groups = taps_ref.shape[0]
+
     def one(g, carry):
-        row = jnp.broadcast_to(rows_ref[pl.ds(g, 1), :], (BLK, 2 * BLK))
-        band_ref[g] = pltpu.roll(row, 0, 1, stride=1, stride_axis=0).astype(BF16)
+        row = jnp.broadcast_to(taps_ref[pl.ds(g, 1), :], (BLK, LM))
+        wide = jnp.concatenate([row, jnp.zeros((BLK, BLK), F32)], 1)
+        wide = pltpu.roll(wide, 0, 1, stride=1, stride_axis=0)
+        band_ref[groups + g] = wide.astype(BF16)
+        band_ref[g, :, 0:BLK] = wide[:, BLK:].T.astype(BF16)
+        band_ref[g, :, BLK:] = wide[:, 0:BLK].T.astype(BF16)
         return carry
 
-    lax.fori_loop(0, rows_ref.shape[0], one, 0)
+    lax.fori_loop(0, groups, one, 0)
 
 
 def apply_band(band_ref, first, source_ref, row0):
@@ -44,7 +48,7 @@
     return jnp.concatenate(totals, 1)
 
 
-def mixer(pre, cot, taps, band, mix, gp, ext, feat, gext, gfext, gft, ptail, ghead, gtail, send, recv):
+def mixer(pre, cot, taps, band, mix, gp, ext, feat, gext, gfext, gft, ptail, ghead, gtail, send, recv, hooks=()):
     tok, ch = pre.shape[1], pre.shape[2]
     n = lax.axis_size("seq")
     me = lax.axis_index("seq")
@@ -79,6 +83,7 @@
     gated_copy = remote(gext.at[pl.ds(tok, BLK), :], gext.at[pl.ds(0, BLK), :], 1, after)
     gated_copy.start()
 
+    hooks[0]()
     tail_copy.wait_recv()
     for j in range(3):
         ext[j, 0:8, :] = jnp.where(first, 0.0, ptail[j].astype(F32)[8:16])
@@ -101,6 +106,7 @@
         gft[0, lo : lo + BLK, :] = (cot[lo : lo + BLK, :].astype(F32) * filt).astype(BF16).astype(F32)
 
     grad_kv(0)
+    hooks[1]()
     gated_copy.wait_recv()
 
     @pl.when(first)
@@ -113,6 +119,7 @@
     head_copy = remote(ghead.at[0], ghead.at[1], 3, before)
     head_copy.start()
     forward(BLK)
+    hooks[2]()
     filt_copy.wait_recv()
     gfext[tok : tok + BLK, :] = jnp.where(last, 0.0, gtail[...].astype(F32)).astype(BF16)
     grad_kv(BLK)
@@ -144,10 +151,53 @@
     ]
 
 
+class Gather:
+    def __init__(self, ring, pair, block, slot, device, send, recv):
+        self.ring, self.pair, self.block, self.slot, self.device = ring, pair, block, slot, device
+        self.send, self.recv = send, recv
+
+    def at(self, step, flip):
+        ring = lax.rem(self.ring + step + 4, 4)
+        return ring, (1 - self.pair if flip else self.pair)
+
+    def source(self, i):
+        where = ((0, 1), (-1, 0), (1, 0), (-1, 1), (1, 1), (2, 0), (2, 1))[i]
+        return self.slot(*self.at(*where))
+
+    def copy(self, i):
+        what, to = (
+            ((0, 0), (0, 1)), ((0, 0), (1, 0)), ((0, 0), (-1, 0)), ((0, 1), (1, 0)),
+            ((0, 1), (-1, 0)), ((-1, 0), (1, 0)), ((1, 1), (-1, 0)),
+        )[i]
+        block = self.block(self.slot(*self.at(*what)))
+        return pltpu.make_async_remote_copy(
+            src_ref=block, dst_ref=block, send_sem=self.send.at[i], recv_sem=self.recv.at[i],
+            device_id=self.device(*self.at(*to)), device_id_type=MESH,
+        )
+
+    def start(self):
+        for i in (1, 2, 0):
+            self.copy(i).start()
+
+    def arrive(self, i):
+        block = self.block(self.source(i))
+        pltpu.make_async_remote_copy(
+            src_ref=block, dst_ref=block, send_sem=self.send.at[i], recv_sem=self.recv.at[i],
+            device_id=self.device(*self.at(0, 1)), device_id_type=MESH,
+        ).wait_recv()
+        for following in {0: (3, 4), 1: (5,), 4: (6,)}.get(i, ()):
+            self.copy(following).start()
+        return self.source(i)
+
+    def settle(self):
+        for i in range(7):
+            self.copy(i).wait_send()
+
+
 def whole_kernel(
-    act, gain, weight, cot, taps, rows, mix, grad_in, grad_proj,
+    act, gain, weight, cot, taps, medium, mix, grad_in, grad_proj,
     ag, w, acc, ssq, inv, pre, gp, col, cols_t, gp_all, total, sib_out, sib_in, pair_out, pair_in, part, stats,
-    load_sem, w_sem, ag_sem, fwd_sem, col_sem, colf_sem, gp_sem, sib_sem, pair_sem, stat_sem, statp_sem,
+    load_sem, w_sem, ag_sem, fwd_sem, turn_sem, col_sem, colf_sem, gp_sem, sib_sem, pair_sem, stat_sem, statp_sem,
     band, *halo,
 ):
     n_seq, n_tp = lax.axis_size("seq"), lax.axis_size("tp")
@@ -168,9 +218,6 @@
     def tp_peer(k):
         return lax.rem(q + k, chips) * 2 + core
 
-    def tp_source(k):
-        return lax.rem(q + chips - k, chips)
-
     def loop(lo, hi, body):
         def step(i, carry):
             body(i)
@@ -204,42 +251,58 @@
 
     loop(1, 8, greet)
     pl.semaphore_signal(barrier, inc=1, device_id={"seq": s, "tp": sib}, device_id_type=MESH)
+
+    @pl.when(q != s)
+    def _():
+        pl.semaphore_signal(barrier, inc=1, device_id={"seq": q, "tp": 2 * s + core}, device_id_type=MESH)
+
     for copy in loads:
         copy.wait()
-    pl.semaphore_wait(barrier, 15)
-
-    def ag_copy(k):
-        return remote(ag.at[p], ag.at[p], ag_sem, k, {"tp": tp_peer(k)})
-
-    def ag_in(k):
-        slot = tp_source(k) * 2 + core
-        return remote(ag.at[slot], ag.at[slot], ag_sem, k, {"tp": sib})
-
-    def fwd_copy(k):
-        slot = tp_source(k) * 2 + core
-        return remote(ag.at[slot], ag.at[slot], fwd_sem, k, {"tp": sib})
-
-    def fwd_in(k):
-        slot = tp_source(k) * 2 + 1 - core
-        return remote(ag.at[slot], ag.at[slot], fwd_sem, k, {"tp": sib})
-
-    def col_send(to):
+    pl.semaphore_wait(barrier, 15 + jnp.where(q != s, 1, 0))
+
+    y, z_lo = q // 2, lax.rem(q, 2)
+    gather = Gather(
+        y, z_lo, lambda chip: ag.at[chip * 2 + core], lambda r, z: r * 2 + z,
+        lambda r, z: {"tp": (r * 2 + z) * 2 + core}, ag_sem.at[0], ag_sem.at[1],
+    )
+    gather.start()
+
+    def turned_copy():
         return pltpu.make_async_remote_copy(
-            src_ref=ag.at[to * 2 + core, pl.ds(0, tok), :], dst_ref=col.at[s, core],
-            send_sem=col_sem.at[0, to], recv_sem=col_sem.at[1, s],
-            device_id={"seq": to}, device_id_type=MESH,
+            src_ref=ag.at[p, pl.ds(0, tok), :], dst_ref=col.at[s, core],
+            send_sem=turn_sem.at[0], recv_sem=turn_sem.at[1],
+            device_id={"seq": q, "tp": 2 * s + core}, device_id_type=MESH,
         )
 
-    def col_in(source):
-        return pltpu.make_async_remote_copy(
-            src_ref=col.at[source, core], dst_ref=col.at[source, core],
-            send_sem=col_sem.at[0, source], recv_sem=col_sem.at[1, source],
-            device_id={"seq": source}, device_id_type=MESH,
-        )
-
-    loop(1, chips, lambda k: ag_copy(k).start())
-    build_bands(rows, band)
-
+    @pl.when(q != s)
+    def _():
+        turned_copy().start()
+
+    @pl.when(q == s)
+    def _():
+        col[s, core] = ag[p, 0:tok, :]
+
+    columns = Gather(
+        y, z_lo, lambda chip: col.at[chip, core], lambda r, z: r * 2 + z,
+        lambda r, z: {"tp": (r * 2 + z) * 2 + core}, col_sem.at[0], col_sem.at[1],
+    )
+
+    def fwd_copy(i, chip):
+        slot = chip * 2 + core
+        return remote(ag.at[slot], ag.at[slot], fwd_sem, i, {"tp": sib})
+
+    def fwd_in(i, chip):
+        slot = chip * 2 + 1 - core
+        return remote(ag.at[slot], ag.at[slot], fwd_sem, i, {"tp": sib})
+
+    def colf_copy(i, chip):
+        return remote(col.at[chip, core], col.at[chip, core], colf_sem, i, {"tp": sib})
+
+    def colf_in(i, chip):
+        return remote(col.at[chip, 1 - core], col.at[chip, 1 - core], colf_sem, i, {"tp": sib})
+
+    fwd_copy(7, q).start()
+    build_bands(medium, band)
     acc[...] = jnp.zeros_like(acc)
     ssq[...] = jnp.zeros_like(ssq)
 
@@ -253,23 +316,33 @@
         for j in range(3):
             acc[j] += jnp.dot(scaled, w[j, block_rows(slot), :], preferred_element_type=F32)
 
-    def gather(k):
-        @pl.when(k > 0)
-        def _():
-            ag_in(k).wait_recv()
-
-        source = tp_source(k)
-        fwd_copy(k).start()
-
-        @pl.when(source != s)
-        def _():
-            col_send(source).start()
-
-        absorb(source * 2 + core)
-        fwd_in(k).wait_recv()
-        absorb(source * 2 + 1 - core)
-
-    loop(0, chips, gather)
+    def absorb_both(i, chip):
+        absorb(chip * 2 + core)
+        fwd_in(i, chip).wait_recv()
+        absorb(chip * 2 + 1 - core)
+
+    def take(i):
+        chip = gather.arrive(i)
+        fwd_copy(i, chip).start()
+        return chip
+
+    def pass_on(i):
+        colf_copy(i, columns.arrive(i)).start()
+
+    absorb_both(7, q)
+    for i in (1, 2, 0, 4, 3):
+        absorb_both(i, take(i))
+
+    @pl.when(q != s)
+    def _():
+        turned_copy().wait_recv()
+
+    columns.start()
+    colf_copy(7, q).start()
+    five = take(5)
+    six = take(6)
+    absorb_both(5, five)
+    absorb_both(6, six)
 
     inv[...] = jnp.broadcast_to(
         lax.rsqrt(jnp.sum(ssq[...], axis=1, keepdims=True) * (1.0 / width) + EPS), inv.shape
@@ -277,21 +350,25 @@
     for j in range(3):
         pre[j] = (acc[j] * inv[:, 0:1]).astype(BF16)
 
-    mixer(pre, cot, taps, band, mix, gp, *halo)
-
-    def gp_copy(k):
-        return remote(gp_all.at[s], gp_all.at[s], gp_sem, k, {"seq": lax.rem(s + k, n_seq)})
-
-    def gp_in(k):
-        slot = lax.rem(s + n_seq - k, n_seq)
-        return remote(gp_all.at[slot], gp_all.at[slot], gp_sem, k, {"seq": slot})
-
+    mixer(
+        pre, cot, taps, band, mix, gp, *halo,
+        hooks=(
+            lambda: (pass_on(1), pass_on(2)),
+            lambda: pass_on(0),
+            lambda: (pass_on(4), pass_on(3)),
+        ),
+    )
+
+    seq_gather = Gather(
+        lax.rem(s, 4), s // 4, lambda slot: gp_all.at[slot], lambda r, z: z * 4 + r,
+        lambda r, z: {"seq": z * 4 + r}, gp_sem.at[0], gp_sem.at[1],
+    )
     stat = jnp.zeros((tok, ch), F32)
     for j in range(3):
         value = gp[j].astype(F32)
         gp_all[s, j] = (value * inv[:, 0:1]).astype(BF16)
         stat += value * pre[j].astype(F32)
-    loop(1, n_seq, lambda k: gp_copy(k).start())
+    seq_gather.start()
 
     eye = lax.broadcasted_iota(jnp.int32, (128, 128), 0) == lax.broadcasted_iota(jnp.int32, (128, 128), 1)
 
@@ -343,33 +420,27 @@
 
     loop(1, chips, lambda k: stat_copy(k).start())
 
-    def colf_copy(source):
-        return remote(col.at[source, core], col.at[source, core], colf_sem, source, {"tp": sib})
-
-    def colf_in(source):
-        return remote(col.at[source, 1 - core], col.at[source, 1 - core], colf_sem, source, {"tp": sib})
-
-    def seq_source(k):
-        return lax.rem(s + n_seq - k, n_seq)
-
-    def turn(source):
+    def turn(chip):
         for half in range(2):
-            cols_t[source, half * own : half * own + own, :] = col[source, half].T
-
-    def pass_on(k):
-        col_in(seq_source(k)).wait_recv()
-        colf_copy(seq_source(k)).start()
-
-    for half in range(2):
-        col[s, half] = ag[s * 2 + half, 0:tok, :]
-    turn(s)
-    loop(1, n_seq, pass_on)
-
-    def turn_next(k):
-        colf_in(seq_source(k)).wait_recv()
-        turn(seq_source(k))
-
-    loop(1, n_seq, turn_next)
+            cols_t[chip, half * own : half * own + own, :] = col[chip, half].T
+
+    def turn_in(i, chip):
+        colf_in(i, chip).wait_recv()
+        turn(chip)
+
+    def product(source, begin=False):
+        for j in range(3):
+            term = jnp.dot(cols_t[source], gp_all[source, j], preferred_element_type=F32)
+            total[j] = term if begin else total[j] + term
+
+    pass_on(5)
+    pass_on(6)
+    turn_in(7, q)
+    for i in range(7):
+        turn_in(i, columns.source(i))
+    product(s, True)
+    for i in (1, 2, 0, 4, 3):
+        product(seq_gather.arrive(i))
 
     sib_copy(chips - 1).wait_recv()
     summed = part[(chips - 1) % 2] + sib_in[chips - 1].astype(F32)
@@ -390,24 +461,8 @@
         scaled = ag[p, r, :].astype(F32) * rms
         grad_in[r, :] = (rms * (own_gain * part[0, r, :] - scaled * stat_col)).astype(BF16)
 
-    total[...] = jnp.zeros_like(total)
-
-    def product(k):
-        @pl.when(k > 0)
-        def _():
-            gp_in(k).wait_recv()
-
-        source = seq_source(k)
-
-        def piece(c):
-            r = pl.ds(pl.multiple_of(c * 128, 128), 128)
-            left = cols_t[source, r, :]
-            for j in range(3):
-                total[j, r, :] += jnp.dot(left, gp_all[source, j], preferred_element_type=F32)
-
-        loop(0, 2 * own // 128, piece)
-
-    loop(0, n_seq, product)
+    for i in (5, 6):
+        product(seq_gather.arrive(i))
     for c in range(2 * own // 128):
         lane = (c * 128) % own
         g = ag[s * 2 + c * 128 // own, tok : tok + 16, lane : lane + 128].astype(F32)[0:1]
@@ -418,28 +473,24 @@
     def settle(k):
         @pl.when(k > 0)
         def _():
-            ag_copy(k).wait_send()
-            gp_copy(k).wait_send()
             stat_copy(k).wait_send()
             pair_copy(k - 1).wait_send()
 
-        fwd_copy(k).wait_send()
         sib_copy(k).wait_send()
 
-        @pl.when(k != s)
-        def _():
-            col_send(k).wait_send()
-            colf_copy(k).wait_send()
-
     loop(0, chips, settle)
+    for group in (gather, columns, seq_gather):
+        group.settle()
+    for i in range(8):
+        chip = q if i == 7 else gather.source(i)
+        fwd_copy(i, chip).wait_send()
+        colf_copy(i, chip).wait_send()
+
+    @pl.when(q != s)
+    def _():
+        turned_copy().wait_send()
+
     stat_sib.wait_send()
-
-
-def band_rows(medium_taps):
-    zero = jnp.zeros_like(medium_taps)
-    forward = jnp.concatenate([zero[:, :1], medium_taps[:, ::-1], zero[:, 1:]], 1)
-    backward = jnp.concatenate([medium_taps, zero], 1)
-    return jnp.concatenate([forward, backward], 0)
 
 
 def per_device(activations, norm_gain, in_proj, short_taps, medium_taps, cotangent):
@@ -479,7 +530,7 @@
             pltpu.VMEM((2 + chips, 8, 128), F32),
             pltpu.SemaphoreType.DMA((2,)),
             pltpu.SemaphoreType.DMA((n_tp,)),
-            sems(chips), sems(chips), sems(n_seq), sems(n_seq), sems(n_seq), sems(chips), sems(chips), sems(chips), sems(1),
+            sems(7), sems(8), pltpu.SemaphoreType.DMA((2,)), sems(7), sems(8), sems(7), sems(chips), sems(chips), sems(chips), sems(1),
         ] + mixer_scratch(tok, ch),
         compiler_params=pltpu.CompilerParams(
             collective_id=0, has_side_effects=True, vmem_limit_bytes=60 * 2**20
@@ -490,7 +541,7 @@
         jnp.transpose(in_proj, (1, 0, 2)),
         cotangent,
         short_taps,
-        band_rows(medium_taps),
+        medium_taps,
     )
     return mix, grad_in, jnp.transpose(grad_proj, (1, 0, 2))
 

time: 164 us -> 121 us (0.74)
  the two profiles are of different devices: /device:TPU:6 before, /device:TPU:98 now
where the time goes in v3:
time: 121 us; the launch traced here: 120 us
  Pallas kernels  113 us (93%)
  local copies, waits for them, and re-layouts  7.18 us (6%)
    pallas_call x1, Pallas kernels, per_device(): pl.pallas_call(whole_kernel, out_shape=(jax.ShapeDtypeStruct((tok, ch), B...  113 us
    unnamed x3, local copies, waits for them, and re-layouts  5.89 us

profile of v3, /device:TPU:98, one launch (start us, length us, event | category | flops | bytes accessed | tf_op | source)
XLA Modules:
  0.0 120.5 jit_solution(931345301055466079)
XLA Ops:
  0.6 1.3 %broadcast_in_dim.2.gain = bf16[16,512]{1,0:T(8,128)(2,1)} broadcast(bf16[512]{0:T(512)(128)(2,1)} %param.7), dimensions={1} | broadcast | bytes 17408 | tf_op jit(solution)/shard_map/broadcast_in_dim | solution.py:540
  1.9 112.7 %shard_map.85 = (bf16[256,256]{1,0:T(8,128)(2,1)}, bf16[256,512]{1,0:T(8,128)(2,1)}, bf16[3,1024,256]{2,1,0:T(8,128)(2,1)}) custom-call(bf16[256,512]{1,0:T(8,128)(2,1)} %act.1, bf16[16,512]{1,0:T(8,128)(2,1)} %broadcast_in_dim.2.gain, bf16[3,8192,256]{2,1,0:T(8,128)(2,1)} %bitcast.2, bf16[256,256]{1,0:T(8,128)(2,1)} %cot.1, f32[3,3,256]{2,1,0:T(4,128)} %taps.1, ...), custom_call_target="tpu_custom_call" | custom-call | tf_op jit(solution)/shard_map/pallas_call | solution.py:504
  114.6 1.6 %copy.12 = bf16[256,256]{1,0:T(8,128)(2,1)} copy(bf16[256,256]{1,0:T(8,128)(2,1)} %get-tuple-element.12) | data formatting | bytes 262144
  116.1 1.7 %copy.13 = bf16[256,512]{1,0:T(8,128)(2,1)} copy(bf16[256,512]{1,0:T(8,128)(2,1)} %get-tuple-element.13) | data formatting | bytes 524288
  117.8 2.7 %copy.14 = bf16[1024,3,256]{2,0,1:T(8,128)(2,1)} copy(bf16[1024,3,256]{2,0,1:T(8,128)(2,1)} %bitcast.3) | data formatting | bytes 3145728

commit v4 on v3

--- a/solution.py
+++ b/solution.py
@@ -48,7 +48,7 @@
     return jnp.concatenate(totals, 1)
 
 
-def mixer(pre, cot, taps, band, mix, gp, ext, feat, gext, gfext, gft, ptail, ghead, gtail, send, recv, hooks=()):
+def mixer(pre, cot, taps, band, mix, gp, ext, feat, gext, gfext, gft, ptail, ghead, gtail, send, recv):
     tok, ch = pre.shape[1], pre.shape[2]
     n = lax.axis_size("seq")
     me = lax.axis_index("seq")
@@ -83,7 +83,6 @@
     gated_copy = remote(gext.at[pl.ds(tok, BLK), :], gext.at[pl.ds(0, BLK), :], 1, after)
     gated_copy.start()
 
-    hooks[0]()
     tail_copy.wait_recv()
     for j in range(3):
         ext[j, 0:8, :] = jnp.where(first, 0.0, ptail[j].astype(F32)[8:16])
@@ -106,7 +105,6 @@
         gft[0, lo : lo + BLK, :] = (cot[lo : lo + BLK, :].astype(F32) * filt).astype(BF16).astype(F32)
 
     grad_kv(0)
-    hooks[1]()
     gated_copy.wait_recv()
 
     @pl.when(first)
@@ -119,7 +117,6 @@
     head_copy = remote(ghead.at[0], ghead.at[1], 3, before)
     head_copy.start()
     forward(BLK)
-    hooks[2]()
     filt_copy.wait_recv()
     gfext[tok : tok + BLK, :] = jnp.where(last, 0.0, gtail[...].astype(F32)).astype(BF16)
     grad_kv(BLK)
@@ -196,8 +193,8 @@
 
 def whole_kernel(
     act, gain, weight, cot, taps, medium, mix, grad_in, grad_proj,
-    ag, w, acc, ssq, inv, pre, gp, col, cols_t, gp_all, total, sib_out, sib_in, pair_out, pair_in, part, stats,
-    load_sem, w_sem, ag_sem, fwd_sem, turn_sem, col_sem, colf_sem, gp_sem, sib_sem, pair_sem, stat_sem, statp_sem,
+    ag, w, acc, ssq, inv, pre, gp, col, cols_t, gp_all, total, sib_out, sib_in, pair_out, pair_in, part, kept, stats,
+    load_sem, w_sem, ag_sem, fwd_sem, col_sem, spread_sem, colf_sem, gp_sem, sib_sem, pair_sem, stat_sem, statp_sem,
     band, *halo,
 ):
     n_seq, n_tp = lax.axis_size("seq"), lax.axis_size("tp")
@@ -252,13 +249,9 @@
     loop(1, 8, greet)
     pl.semaphore_signal(barrier, inc=1, device_id={"seq": s, "tp": sib}, device_id_type=MESH)
 
-    @pl.when(q != s)
-    def _():
-        pl.semaphore_signal(barrier, inc=1, device_id={"seq": q, "tp": 2 * s + core}, device_id_type=MESH)
-
     for copy in loads:
         copy.wait()
-    pl.semaphore_wait(barrier, 15 + jnp.where(q != s, 1, 0))
+    pl.semaphore_wait(barrier, 15)
 
     y, z_lo = q // 2, lax.rem(q, 2)
     gather = Gather(
@@ -267,25 +260,46 @@
     )
     gather.start()
 
-    def turned_copy():
+    z_hi, x_at = s // 4, lax.rem(s, 4)
+    def col_send(to):
         return pltpu.make_async_remote_copy(
-            src_ref=ag.at[p, pl.ds(0, tok), :], dst_ref=col.at[s, core],
-            send_sem=turn_sem.at[0], recv_sem=turn_sem.at[1],
-            device_id={"seq": q, "tp": 2 * s + core}, device_id_type=MESH,
+            src_ref=ag.at[to * 2 + core, pl.ds(0, tok), :], dst_ref=col.at[s, core],
+            send_sem=col_sem.at[0, to], recv_sem=col_sem.at[1, s],
+            device_id={"seq": to}, device_id_type=MESH,
         )
 
-    @pl.when(q != s)
-    def _():
-        turned_copy().start()
-
-    @pl.when(q == s)
-    def _():
-        col[s, core] = ag[p, 0:tok, :]
-
-    columns = Gather(
-        y, z_lo, lambda chip: col.at[chip, core], lambda r, z: r * 2 + z,
-        lambda r, z: {"tp": (r * 2 + z) * 2 + core}, col_sem.at[0], col_sem.at[1],
-    )
+    def col_in(source):
+        return pltpu.make_async_remote_copy(
+            src_ref=col.at[source, core], dst_ref=col.at[source, core],
+            send_sem=col_sem.at[0, source], recv_sem=col_sem.at[1, source],
+            device_id={"seq": source}, device_id_type=MESH,
+        )
+
+    def col_due(chip):
+        near = chip // 4 == z_hi
+        return (near & (lax.rem(chip, 4) != x_at)) | (~near & (lax.rem(chip + y, 4) == x_at))
+
+    def col_start(chip):
+        @pl.when(col_due(chip))
+        def _():
+            col_send(chip).start()
+
+    def fetched(step):
+        return (1 - z_hi) * 4 + lax.rem(x_at + y + step + 4, 4)
+
+    def spread(i):
+        step, part_rows, to = (
+            (0, pl.ds(0, tok), 1), (0, pl.ds(0, tok), 3), (-1, pl.ds(0, tok // 2), 1), (1, pl.ds(tok // 2, tok // 2), 3),
+        )[i]
+        block = col.at[fetched(step), core, part_rows, :]
+        return remote(block, block, spread_sem, i, {"tp": (lax.rem(y + to, 4) * 2 + z_lo) * 2 + core})
+
+    def spread_in(i):
+        step, part_rows = (
+            (-1, pl.ds(0, tok)), (1, pl.ds(0, tok)), (2, pl.ds(0, tok // 2)), (2, pl.ds(tok // 2, tok // 2)),
+        )[i]
+        block = col.at[fetched(step), core, part_rows, :]
+        return remote(block, block, spread_sem, i, {"tp": sib})
 
     def fwd_copy(i, chip):
         slot = chip * 2 + core
@@ -295,12 +309,13 @@
         slot = chip * 2 + 1 - core
         return remote(ag.at[slot], ag.at[slot], fwd_sem, i, {"tp": sib})
 
-    def colf_copy(i, chip):
-        return remote(col.at[chip, core], col.at[chip, core], colf_sem, i, {"tp": sib})
-
-    def colf_in(i, chip):
-        return remote(col.at[chip, 1 - core], col.at[chip, 1 - core], colf_sem, i, {"tp": sib})
-
+    def colf_copy(source):
+        return remote(col.at[source, core], col.at[source, core], colf_sem, source, {"tp": sib})
+
+    def colf_in(source):
+        return remote(col.at[source, 1 - core], col.at[source, 1 - core], colf_sem, source, {"tp": sib})
+
+    col_start(q)
     fwd_copy(7, q).start()
     build_bands(medium, band)
     acc[...] = jnp.zeros_like(acc)
@@ -324,21 +339,13 @@
     def take(i):
         chip = gather.arrive(i)
         fwd_copy(i, chip).start()
+        col_start(chip)
         return chip
-
-    def pass_on(i):
-        colf_copy(i, columns.arrive(i)).start()
 
     absorb_both(7, q)
     for i in (1, 2, 0, 4, 3):
         absorb_both(i, take(i))
 
-    @pl.when(q != s)
-    def _():
-        turned_copy().wait_recv()
-
-    columns.start()
-    colf_copy(7, q).start()
     five = take(5)
     six = take(6)
     absorb_both(5, five)
@@ -352,11 +359,6 @@
 
     mixer(
         pre, cot, taps, band, mix, gp, *halo,
-        hooks=(
-            lambda: (pass_on(1), pass_on(2)),
-            lambda: pass_on(0),
-            lambda: (pass_on(4), pass_on(3)),
-        ),
     )
 
     seq_gather = Gather(
@@ -392,16 +394,30 @@
     def sib_copy(i):
         return remote(sib_out.at[i], sib_in.at[i], sib_sem, i, {"tp": sib})
 
+    def chunk_y(i):
+        return lax.rem(y + 2 + i, 4)
+
     def pair_copy(i):
-        return remote(pair_out.at[i], pair_in.at[i], pair_sem, i, {"tp": tp_peer(i + 1)})
+        return remote(pair_out.at[i], pair_in.at[i], pair_sem, i, {"tp": (chunk_y(i) * 2 + z_lo) * 2 + core})
+
+    def across():
+        return remote(pair_out.at[2], pair_in.at[2], pair_sem, 2, {"tp": (y * 2 + 1 - z_lo) * 2 + core})
 
     def finish(i):
         sib_copy(i).wait_recv()
-        pair_out[i] = (part[lax.rem(i, 2)] + sib_in[i].astype(F32)).astype(BF16)
-        pair_copy(i).start()
+        both = part[lax.rem(i, 2)] + sib_in[i].astype(F32)
+
+        @pl.when(lax.rem(i, 4) == 2)
+        def _():
+            kept[i // 4] = both
+
+        @pl.when(lax.rem(i, 4) != 2)
+        def _():
+            pair_out[i] = both.astype(BF16)
+            pair_copy(i).start()
 
     def reduce(i):
-        chip = lax.rem(q + 1 + i, chips)
+        chip = chunk_y(i) * 2 + jnp.where(i < 4, 1 - z_lo, z_lo)
         sib_out[i] = partial(block_rows(chip * 2 + 1 - core)).astype(BF16)
         sib_copy(i).start()
         part[lax.rem(i, 2)] = partial(block_rows(chip * 2 + core))
@@ -411,6 +427,19 @@
             finish(i - 1)
 
     loop(0, chips, reduce)
+    finish(chips - 1)
+    for i in (1, 2, 0):
+        seq_gather.arrive(i)
+    for i in (0, 3, 1):
+        pair_copy(i).wait_recv()
+    pair_out[2] = (
+        kept[0] + pair_in[0].astype(F32) + pair_in[1].astype(F32) + pair_in[3].astype(F32)
+    ).astype(BF16)
+    across().start()
+    col_in(fetched(0)).wait_recv()
+    for i in range(2):
+        spread(i).start()
+
 
     stat_sib.wait_recv()
     stats[2] = stats[0] + stats[1]
@@ -423,34 +452,52 @@
     def turn(chip):
         for half in range(2):
             cols_t[chip, half * own : half * own + own, :] = col[chip, half].T
-
-    def turn_in(i, chip):
-        colf_in(i, chip).wait_recv()
-        turn(chip)
 
     def product(source, begin=False):
         for j in range(3):
             term = jnp.dot(cols_t[source], gp_all[source, j], preferred_element_type=F32)
             total[j] = term if begin else total[j] + term
 
-    pass_on(5)
-    pass_on(6)
-    turn_in(7, q)
-    for i in range(7):
-        turn_in(i, columns.source(i))
+    for half in range(2):
+        col[s, half] = ag[s * 2 + half, 0:tok, :]
+
+    def pass_on(k):
+        source = z_hi * 4 + lax.rem(x_at + k, 4)
+        col_in(source).wait_recv()
+        colf_copy(source).start()
+
+    def turn_in(k):
+        source = lax.rem(s + n_seq - k, n_seq)
+        colf_in(source).wait_recv()
+        turn(source)
+
+    loop(1, 4, pass_on)
+    turn(s)
+    for i in (4, 3):
+        seq_gather.arrive(i)
+    for i in range(2):
+        spread_in(i).wait_recv()
+        spread(i + 2).start()
+    for step in (0, -1, 1):
+        colf_copy(fetched(step)).start()
+    for i in (2, 3):
+        spread_in(i).wait_recv()
+    colf_copy(fetched(2)).start()
+    loop(1, n_seq, turn_in)
     product(s, True)
     for i in (1, 2, 0, 4, 3):
-        product(seq_gather.arrive(i))
-
-    sib_copy(chips - 1).wait_recv()
-    summed = part[(chips - 1) % 2] + sib_in[chips - 1].astype(F32)
-    part[0] = summed
+        product(seq_gather.source(i))
 
     def collect(k):
-        pair_copy(k - 1).wait_recv()
         stat_copy(k).wait_recv()
-        part[0] += pair_in[k - 1].astype(F32)
-
+
+    for i in (4, 5, 7):
+        pair_copy(i).wait_recv()
+    across().wait_recv()
+    part[0] = (
+        kept[1] + pair_in[4].astype(F32) + pair_in[5].astype(F32)
+        + pair_in[7].astype(F32) + pair_in[2].astype(F32)
+    )
     loop(1, chips, collect)
     stat_rows = sum(stats[2 + k] for k in range(chips)) * (1.0 / width)
     own_gain = ag[p, tok : tok + 16, :].astype(F32)[0:1]
@@ -474,22 +521,30 @@
         @pl.when(k > 0)
         def _():
             stat_copy(k).wait_send()
-            pair_copy(k - 1).wait_send()
+
+        @pl.when(lax.rem(k, 4) != 2)
+        def _():
+            pair_copy(k).wait_send()
 
         sib_copy(k).wait_send()
 
+        @pl.when(col_due(k))
+        def _():
+            col_send(k).wait_send()
+
+        @pl.when(k != s)
+        def _():
+            colf_copy(k).wait_send()
+
     loop(0, chips, settle)
-    for group in (gather, columns, seq_gather):
+    across().wait_send()
+    for i in range(4):
+        spread(i).wait_send()
+    for group in (gather, seq_gather):
         group.settle()
     for i in range(8):
         chip = q if i == 7 else gather.source(i)
         fwd_copy(i, chip).wait_send()
-        colf_copy(i, chip).wait_send()
-
-    @pl.when(q != s)
-    def _():
-        turned_copy().wait_send()
-
     stat_sib.wait_send()
 
 
@@ -527,10 +582,11 @@
             pltpu.VMEM((chips, tok, own), BF16),
             pltpu.VMEM((chips, tok, own), BF16),
             pltpu.VMEM((2, tok, own), F32),
+            pltpu.VMEM((2, tok, own), F32),
             pltpu.VMEM((2 + chips, 8, 128), F32),
             pltpu.SemaphoreType.DMA((2,)),
             pltpu.SemaphoreType.DMA((n_tp,)),
-            sems(7), sems(8), pltpu.SemaphoreType.DMA((2,)), sems(7), sems(8), sems(7), sems(chips), sems(chips), sems(chips), sems(1),
+            sems(7), sems(8), sems(n_seq), sems(4), sems(n_seq), sems(7), sems(chips), sems(chips), sems(chips), sems(1),
         ] + mixer_scratch(tok, ch),
         compiler_params=pltpu.CompilerParams(
             collective_id=0, has_side_effects=True, vmem_limit_bytes=60 * 2**20

time: 121 us -> 110 us (0.909)
  the two profiles are of different devices: /device:TPU:98 before, /device:TPU:1 now
where the time goes in v4:
time: 110 us
  Pallas kernels  102 us (93%)
  local copies, waits for them, and re-layouts  7.18 us (7%)
    pallas_call x1, Pallas kernels, per_device(): pl.pallas_call(whole_kernel, out_shape=(jax.ShapeDtypeStruct((tok, ch), B...  102 us
    unnamed x3, local copies, waits for them, and re-layouts  5.89 us

profile of v4, /device:TPU:1, one launch (start us, length us, event | category | flops | bytes accessed | tf_op | source)
XLA Modules:
  0.0 109.5 jit_solution(5306005521619330500)
XLA Ops:
  0.6 1.3 %broadcast_in_dim.2.gain = bf16[16,512]{1,0:T(8,128)(2,1)} broadcast(bf16[512]{0:T(512)(128)(2,1)} %param.7), dimensions={1} | broadcast | bytes 17408 | tf_op jit(solution)/shard_map/broadcast_in_dim | solution.py:596
  1.9 101.7 %shard_map.85 = (bf16[256,256]{1,0:T(8,128)(2,1)}, bf16[256,512]{1,0:T(8,128)(2,1)}, bf16[3,1024,256]{2,1,0:T(8,128)(2,1)}) custom-call(bf16[256,512]{1,0:T(8,128)(2,1)} %act.1, bf16[16,512]{1,0:T(8,128)(2,1)} %broadcast_in_dim.2.gain, bf16[3,8192,256]{2,1,0:T(8,128)(2,1)} %bitcast.2, bf16[256,256]{1,0:T(8,128)(2,1)} %cot.1, f32[3,3,256]{2,1,0:T(4,128)} %taps.1, ...), custom_call_target="tpu_custom_call" | custom-call | tf_op jit(solution)/shard_map/pallas_call | solution.py:559
  103.7 1.6 %copy.12 = bf16[256,256]{1,0:T(8,128)(2,1)} copy(bf16[256,256]{1,0:T(8,128)(2,1)} %get-tuple-element.12) | data formatting | bytes 262144
  105.2 1.7 %copy.13 = bf16[256,512]{1,0:T(8,128)(2,1)} copy(bf16[256,512]{1,0:T(8,128)(2,1)} %get-tuple-element.13) | data formatting | bytes 524288
  106.9 2.7 %copy.14 = bf16[1024,3,256]{2,0,1:T(8,128)(2,1)} copy(bf16[1024,3,256]{2,0,1:T(8,128)(2,1)} %bitcast.3) | data formatting | bytes 3145728

commit v5 on v4

--- a/solution.py
+++ b/solution.py
@@ -371,6 +371,10 @@
         gp_all[s, j] = (value * inv[:, 0:1]).astype(BF16)
         stat += value * pre[j].astype(F32)
     seq_gather.start()
+    col_in(fetched(0)).wait_recv()
+    for i in range(2):
+        spread(i).start()
+
 
     eye = lax.broadcasted_iota(jnp.int32, (128, 128), 0) == lax.broadcasted_iota(jnp.int32, (128, 128), 1)
 
@@ -428,6 +432,9 @@
 
     loop(0, chips, reduce)
     finish(chips - 1)
+    for i in range(2):
+        spread_in(i).wait_recv()
+        spread(i + 2).start()
     for i in (1, 2, 0):
         seq_gather.arrive(i)
     for i in (0, 3, 1):
@@ -436,10 +443,6 @@
         kept[0] + pair_in[0].astype(F32) + pair_in[1].astype(F32) + pair_in[3].astype(F32)
     ).astype(BF16)
     across().start()
-    col_in(fetched(0)).wait_recv()
-    for i in range(2):
-        spread(i).start()
-
 
     stat_sib.wait_recv()
     stats[2] = stats[0] + stats[1]
@@ -475,9 +478,6 @@
     turn(s)
     for i in (4, 3):
         seq_gather.arrive(i)
-    for i in range(2):
-        spread_in(i).wait_recv()
-        spread(i + 2).start()
     for step in (0, -1, 1):
         colf_copy(fetched(step)).start()
     for i in (2, 3):
@@ -546,6 +546,11 @@
         chip = q if i == 7 else gather.source(i)
         fwd_copy(i, chip).wait_send()
     stat_sib.wait_send()
+
+
+def hand_over(*refs):
+    for source, target in zip(refs[:3], refs[3:]):
+        target[...] = source[...]
 
 
 def per_device(activations, norm_gain, in_proj, short_taps, medium_taps, cotangent):
@@ -599,6 +604,13 @@
         short_taps,
         medium_taps,
     )
+    results = (mix, grad_in, grad_proj)
+    mix, grad_in, grad_proj = pl.pallas_call(
+        hand_over,
+        out_shape=tuple(jax.ShapeDtypeStruct(a.shape, a.dtype) for a in results),
+        in_specs=[vmem] * 3,
+        out_specs=(vmem,) * 3,
+    )(*results)
     return mix, grad_in, jnp.transpose(grad_proj, (1, 0, 2))
 
 

time: 110 us -> 102 us (0.927); the launches traced: 110 us -> 100 us
  local copies, waits for them, and re-layouts: 7.18 us -> 1.29 us
  Pallas kernels: 102 us -> 98.4 us
    pallas_call x1, Pallas kernels: 102 us -> 95.5 us  [per_device(): pl.pallas_call(whole_kernel, out_shape=(jax.ShapeDtypeStruct((tok, ch), B...]
    unnamed x3 -> x0, local copies, waits for them, and re-layouts: 5.89 us -> none
    pallas_call x0 -> x1, Pallas kernels: none -> 2.86 us  [per_device(): pl.pallas_call(hand_over, out_shape=tuple((jax.ShapeDtypeStruct(a.shape,...]
where the time goes in v5:
time: 102 us; the launch traced here: 100 us
  Pallas kernels  98.4 us (96%)
  local copies, waits for them, and re-layouts  1.29 us (1%)
    pallas_call x1, Pallas kernels, per_device(): pl.pallas_call(whole_kernel, out_shape=(jax.ShapeDtypeStruct((tok, ch), B...  95.5 us
    pallas_call x1, Pallas kernels, per_device(): pl.pallas_call(hand_over, out_shape=tuple((jax.ShapeDtypeStruct(a.shape,...  2.86 us

profile of v5, /device:TPU:1, one launch (start us, length us, event | category | flops | bytes accessed | tf_op | source)
XLA Modules:
  0.0 100.3 jit_solution(10800250981814393229)
XLA Ops:
  0.6 1.3 %broadcast_in_dim.2.gain = bf16[16,512]{1,0:T(8,128)(2,1)} broadcast(bf16[512]{0:T(512)(128)(2,1)} %param.7), dimensions={1} | broadcast | bytes 17408 | tf_op jit(solution)/shard_map/broadcast_in_dim | solution.py:601
  1.9 95.5 %shard_map.85 = (bf16[256,256]{1,0:T(8,128)(2,1)}, bf16[256,512]{1,0:T(8,128)(2,1)}, bf16[3,1024,256]{2,1,0:T(8,128)(2,1)}) custom-call(bf16[256,512]{1,0:T(8,128)(2,1)} %act.1, bf16[16,512]{1,0:T(8,128)(2,1)} %broadcast_in_dim.2.gain, bf16[3,8192,256]{2,1,0:T(8,128)(2,1)} %bitcast.2, bf16[256,256]{1,0:T(8,128)(2,1)} %cot.1, f32[3,3,256]{2,1,0:T(4,128)} %taps.1, ...), custom_call_target="tpu_custom_call" | custom-call | tf_op jit(solution)/shard_map/pallas_call | solution.py:564
  97.5 2.9 %shard_map.86 = (bf16[256,256]{1,0:T(8,128)(2,1)}, bf16[256,512]{1,0:T(8,128)(2,1)}, bf16[3,1024,256]{2,1,0:T(8,128)(2,1)}) custom-call(bf16[256,256]{1,0:T(8,128)(2,1)} %get-tuple-element.9.refs_0_, bf16[256,512]{1,0:T(8,128)(2,1)} %get-tuple-element.10.refs_1_, bf16[3,1024,256]{2,1,0:T(8,128)(2,1)} %get-tuple-element.11.refs_2_), custom_call_target="tpu_custom_call" | custom-call | tf_op jit(solution)/shard_map/pallas_call | solution.py:608

commit v6 on v5

--- a/solution.py
+++ b/solution.py
@@ -173,7 +173,7 @@
         )
 
     def start(self):
-        for i in (1, 2, 0):
+        for i in range(3):
             self.copy(i).start()
 
     def arrive(self, i):
@@ -343,8 +343,10 @@
         return chip
 
     absorb_both(7, q)
-    for i in (1, 2, 0, 4, 3):
-        absorb_both(i, take(i))
+    for batch in ((0, 1, 2), (4, 3)):
+        chips_in = [take(i) for i in batch]
+        for i, chip in zip(batch, chips_in):
+            absorb_both(i, chip)
 
     five = take(5)
     six = take(6)

time: 102 us -> 99 us (0.971)
  Pallas kernels: 98.4 us -> 95.9 us
    pallas_call x1, Pallas kernels: 95.5 us -> 93.1 us  [per_device(): pl.pallas_call(whole_kernel, out_shape=(jax.ShapeDtypeStruct((tok, ch), B...]
where the time goes in v6:
time: 99 us; the launch traced here: 97.9 us
  Pallas kernels  95.9 us (97%)
  local copies, waits for them, and re-layouts  1.29 us (1%)
    pallas_call x1, Pallas kernels, per_device(): pl.pallas_call(whole_kernel, out_shape=(jax.ShapeDtypeStruct((tok, ch), B...  93.1 us
    pallas_call x1, Pallas kernels, per_device(): pl.pallas_call(hand_over, out_shape=tuple((jax.ShapeDtypeStruct(a.shape,...  2.86 us

profile of v6, /device:TPU:1, one launch (start us, length us, event | category | flops | bytes accessed | tf_op | source)
XLA Modules:
  0.0 97.9 jit_solution(8092618499482815174)
XLA Ops:
  0.6 1.3 %broadcast_in_dim.2.gain = bf16[16,512]{1,0:T(8,128)(2,1)} broadcast(bf16[512]{0:T(512)(128)(2,1)} %param.7), dimensions={1} | broadcast | bytes 17408 | tf_op jit(solution)/shard_map/broadcast_in_dim | solution.py:603
  1.9 93.1 %shard_map.85 = (bf16[256,256]{1,0:T(8,128)(2,1)}, bf16[256,512]{1,0:T(8,128)(2,1)}, bf16[3,1024,256]{2,1,0:T(8,128)(2,1)}) custom-call(bf16[256,512]{1,0:T(8,128)(2,1)} %act.1, bf16[16,512]{1,0:T(8,128)(2,1)} %broadcast_in_dim.2.gain, bf16[3,8192,256]{2,1,0:T(8,128)(2,1)} %bitcast.2, bf16[256,256]{1,0:T(8,128)(2,1)} %cot.1, f32[3,3,256]{2,1,0:T(4,128)} %taps.1, ...), custom_call_target="tpu_custom_call" | custom-call | tf_op jit(solution)/shard_map/pallas_call | solution.py:566
  95.0 2.9 %shard_map.86 = (bf16[256,256]{1,0:T(8,128)(2,1)}, bf16[256,512]{1,0:T(8,128)(2,1)}, bf16[3,1024,256]{2,1,0:T(8,128)(2,1)}) custom-call(bf16[256,256]{1,0:T(8,128)(2,1)} %get-tuple-element.9.refs_0_, bf16[256,512]{1,0:T(8,128)(2,1)} %get-tuple-element.10.refs_1_, bf16[3,1024,256]{2,1,0:T(8,128)(2,1)} %get-tuple-element.11.refs_2_), custom_call_target="tpu_custom_call" | custom-call | tf_op jit(solution)/shard_map/pallas_call | solution.py:610

commit v7 on v6

--- a/solution.py
+++ b/solution.py
@@ -315,7 +315,6 @@
     def colf_in(source):
         return remote(col.at[source, 1 - core], col.at[source, 1 - core], colf_sem, source, {"tp": sib})
 
-    col_start(q)
     fwd_copy(7, q).start()
     build_bands(medium, band)
     acc[...] = jnp.zeros_like(acc)
@@ -345,6 +344,8 @@
     absorb_both(7, q)
     for batch in ((0, 1, 2), (4, 3)):
         chips_in = [take(i) for i in batch]
+        if 0 in batch:
+            col_start(q)
         for i, chip in zip(batch, chips_in):
             absorb_both(i, chip)
 

time: 99 us -> 96 us (0.970)
  Pallas kernels: 95.9 us -> 92.5 us
    pallas_call x1, Pallas kernels: 93.1 us -> 89.7 us  [per_device(): pl.pallas_call(whole_kernel, out_shape=(jax.ShapeDtypeStruct((tok, ch), B...]
where the time goes in v7:
time: 96 us; the launch traced here: 94.5 us
  Pallas kernels  92.5 us (96%)
  local copies, waits for them, and re-layouts  1.29 us (1%)
    pallas_call x1, Pallas kernels, per_device(): pl.pallas_call(whole_kernel, out_shape=(jax.ShapeDtypeStruct((tok, ch), B...  89.7 us
    pallas_call x1, Pallas kernels, per_device(): pl.pallas_call(hand_over, out_shape=tuple((jax.ShapeDtypeStruct(a.shape,...  2.86 us

profile of v7, /device:TPU:1, one launch (start us, length us, event | category | flops | bytes accessed | tf_op | source)
XLA Modules:
  0.0 94.5 jit_solution(6518743378872147006)
XLA Ops:
  0.6 1.3 %broadcast_in_dim.2.gain = bf16[16,512]{1,0:T(8,128)(2,1)} broadcast(bf16[512]{0:T(512)(128)(2,1)} %param.7), dimensions={1} | broadcast | bytes 17408 | tf_op jit(solution)/shard_map/broadcast_in_dim | solution.py:604
  1.9 89.7 %shard_map.85 = (bf16[256,256]{1,0:T(8,128)(2,1)}, bf16[256,512]{1,0:T(8,128)(2,1)}, bf16[3,1024,256]{2,1,0:T(8,128)(2,1)}) custom-call(bf16[256,512]{1,0:T(8,128)(2,1)} %act.1, bf16[16,512]{1,0:T(8,128)(2,1)} %broadcast_in_dim.2.gain, bf16[3,8192,256]{2,1,0:T(8,128)(2,1)} %bitcast.2, bf16[256,256]{1,0:T(8,128)(2,1)} %cot.1, f32[3,3,256]{2,1,0:T(4,128)} %taps.1, ...), custom_call_target="tpu_custom_call" | custom-call | tf_op jit(solution)/shard_map/pallas_call | solution.py:567
  91.6 2.9 %shard_map.86 = (bf16[256,256]{1,0:T(8,128)(2,1)}, bf16[256,512]{1,0:T(8,128)(2,1)}, bf16[3,1024,256]{2,1,0:T(8,128)(2,1)}) custom-call(bf16[256,256]{1,0:T(8,128)(2,1)} %get-tuple-element.9.refs_0_, bf16[256,512]{1,0:T(8,128)(2,1)} %get-tuple-element.10.refs_1_, bf16[3,1024,256]{2,1,0:T(8,128)(2,1)} %get-tuple-element.11.refs_2_), custom_call_target="tpu_custom_call" | custom-call | tf_op jit(solution)/shard_map/pallas_call | solution.py:611
